TPU v7x, 32 devices: a whole 2x2x4 slice. The times are simulated.
32 devices in a mesh: groups: 2 (over x), blk: 4 (over y, core), dp: 4 (over z).
Axes of the slice: x: 2, y: 2, z: 4, core: 2. Of those that a mesh axis runs over, the one named last changes fastest.
Arguments:
- data: bfloat16 [30720, 768], P(('groups', 'blk', 'dp')), parts along dimension 0, may hold values from -6 to 6
- landmarks: bfloat16 [8192, 768], P(('groups', 'blk')), parts along dimension 0, may hold values from -6 to 6
- basis: bfloat16 [8192, 512], P(('groups', 'blk')), parts along dimension 0, may hold values from -6 to 6
Outputs:
- new_basis: float32 [8192, 512], P(('groups', 'blk')), parts along dimension 0
There are 2 independent parts, one for each index of `groups`. A program takes and returns all parts, laid end to end along the dimension named above; each array names one. Nothing has to cross between parts.
All inputs are finite; a program needn't handle non-finite values.
Results may differ from a plain program's by a relative error of at most 0.0057.
The roundings to bfloat16 on the way count: a program that leaves them out, or rounds other values in their place, can miss the bound.
Values may be sent and summed in bfloat16 or wider, within the bound.
No kernel may reach another device: no remote copies, remote signals or barrier semaphores. Data moves between devices by JAX's collectives and lax.ppermute only.
A program may use at most 128 MiB of HBM per device.

v0:
```python
import functools
import math

import jax
import jax.numpy as jnp
from jax import lax
from jax.experimental import pallas as pl
from jax.experimental.pallas import tpu as pltpu
from jax.sharding import PartitionSpec as P

NORM_EPS = 1e-06
BLOCK = 128
PANEL = 8
HIGHEST = lax.Precision.HIGHEST
SWAP_CORE = [(0, 1), (1, 0), (2, 3), (3, 2)]
SWAP_Y = [(0, 2), (2, 0), (1, 3), (3, 1)]
SWAP_INNER = [(1, 2), (2, 1)]
TO_INNER = [(0, 1), (3, 2)]
TO_OUTER = [(1, 0), (2, 3)]
SWAP_NEAR = [(0, 1), (1, 0), (2, 3), (3, 2)]
ACROSS = [(0, 3), (3, 0), (1, 2), (2, 1)]
SWAP_FAR = [(0, 2), (2, 0), (1, 3), (3, 1)]


def unit_rows(values):
    wide = values.astype(jnp.float32)
    return (wide * lax.rsqrt(jnp.sum(wide * wide, axis=1, keepdims=True) + NORM_EPS)).astype(
        jnp.bfloat16
    )


def kernel_tile(unit_data, unit_marks, exponent_scale):
    scores = lax.dot_general(
        unit_data, unit_marks, (((1,), (1,)), ((), ())), preferred_element_type=jnp.float32
    )
    return jnp.exp(exponent_scale * scores).astype(jnp.bfloat16)


def spread_row(tile, row):
    return jnp.broadcast_to(tile[row : row + 1, :], tile.shape)


def eliminate_panel(square_ref, inverse_ref, panel, low, high):
    size = square_ref.shape[0]
    lane = lax.broadcasted_iota(jnp.int32, (PANEL, size), 1)
    sublane = lax.broadcasted_iota(jnp.int32, (PANEL, size), 0)
    here = pl.ds(pl.multiple_of(panel * PANEL, PANEL), PANEL)

    def columns_of(rows):
        return [jnp.broadcast_to(rows[:, k : k + 1], (PANEL, size)) for k in range(PANEL)]

    head = square_ref[here, :]
    head_columns = columns_of(head)
    scaled, ratios, finished = [], [], jnp.zeros_like(head)
    for k in range(PANEL):
        pivot = spread_row(head_columns[k], k)
        inverse = 1.0 / pivot
        row = jnp.where(lane == k, 1.0, spread_row(head, k))
        finished = jnp.where(sublane == k, row * lax.rsqrt(pivot), finished)
        scaled.append(row * inverse)
        ratios.append({m: spread_row(head_columns[k], m) * inverse for m in range(k + 1, PANEL)})
        for m in range(k + 1, PANEL):
            head_columns[m] = head_columns[m] - head_columns[k] * ratios[k][m]
        head = jnp.where(lane == k, 0.0, head) - head_columns[k] * scaled[k]
    finished = pltpu.roll(finished, panel * PANEL, 1)
    inverse_ref[here, :] = jnp.where(lane <= panel * PANEL + sublane, finished, 0.0)
    weights = [jnp.where((lane <= k) | (lane >= PANEL), scaled[k], 0.0) for k in range(PANEL)]
    for k in reversed(range(PANEL)):
        for m in range(k + 1, PANEL):
            weights[k] = weights[k] - ratios[k][m] * weights[m]
    for g in range(low, high):
        rows = square_ref[PANEL * g : PANEL * (g + 1), :]
        columns = columns_of(rows)
        rows = jnp.where(lane < PANEL, 0.0, rows)
        for k in range(PANEL):
            rows = rows - columns[k] * weights[k]
        square_ref[PANEL * g : PANEL * (g + 1), :] = pltpu.roll(rows, size - PANEL, 1)


def lower_inverse(square_ref, inverse_ref):
    groups = square_ref.shape[0] // PANEL
    spans = 4

    for low in range(0, groups, groups // spans):

        def step(panel, carry):
            eliminate_panel(square_ref, inverse_ref, panel, low, groups)
            return carry

        lax.fori_loop(low, low + groups // spans, step, 0)


def times_transposed(left, right):
    return lax.dot_general(
        left,
        right,
        (((1,), (1,)), ((), ())),
        precision=HIGHEST,
        preferred_element_type=jnp.float32,
    )


def eliminate(scale, left_ref, rows_ref, inverse_ref, square_ref, write):
    order = left_ref.shape[0]
    blocks = order // BLOCK

    def step(position, carry):
        here = pl.ds(pl.multiple_of(position * BLOCK, BLOCK), BLOCK)
        square_ref[...] = left_ref[here, here]
        lower_inverse(square_ref, inverse_ref)
        for b in range(blocks):

            @pl.when(position == b)
            def _():
                now = slice(b * BLOCK, (b + 1) * BLOCK)
                later = slice((b + 1) * BLOCK, order)
                inverse = inverse_ref[...]
                solved = times_transposed(rows_ref[:, now], inverse)
                if b + 1 < blocks:
                    factor = times_transposed(left_ref[later, now], inverse)
                    left_ref[later, later] -= times_transposed(factor, factor)
                    rows_ref[:, later] -= times_transposed(solved, factor)
                write(now, solved * scale)

        return carry

    lax.fori_loop(0, blocks, step, 0)


def whiten_kernel(scale, gram_ref, rows_ref, out_ref, left_ref, moved_ref, inverse_ref, square_ref):
    left_ref[...] = gram_ref[...]
    moved_ref[...] = rows_ref[...]

    def write(now, values):
        out_ref[:, now] = values

    eliminate(scale, left_ref, moved_ref, inverse_ref, square_ref, write)


def first_kernel(gram_ref, rows_ref, out_ref, back_ref, left_ref, moved_ref, inverse_ref, square_ref):
    count, order = rows_ref.shape
    left_ref[...] = gram_ref[...]
    moved_ref[:count, :] = rows_ref[...]
    shape = (order, order)
    moved_ref[count:, :] = jnp.where(
        lax.broadcasted_iota(jnp.int32, shape, 0) == lax.broadcasted_iota(jnp.int32, shape, 1),
        1.0,
        0.0,
    )

    def write(now, values):
        out_ref[:, now] = values[:count]
        back_ref[:, now] = values[count:]

    eliminate(1.0, left_ref, moved_ref, inverse_ref, square_ref, write)


def second_kernel(
    scale, gram_ref, rows_ref, done_ref, solve_ref, out_ref, left_ref, moved_ref, inverse_ref, square_ref
):
    order = rows_ref.shape[1]
    factor = lax.dot_general(
        gram_ref[:, :order],
        solve_ref[...],
        (((1,), (0,)), ((), ())),
        precision=HIGHEST,
        preferred_element_type=jnp.float32,
    )
    left_ref[...] = gram_ref[:, order:] - times_transposed(factor, factor)
    moved_ref[...] = rows_ref[...] - times_transposed(done_ref[...], factor)
    out_ref[:, :order] = done_ref[...] * scale

    def write(now, values):
        out_ref[:, order + now.start : order + now.stop] = values

    eliminate(scale, left_ref, moved_ref, inverse_ref, square_ref, write)


def solve_call(kernel, out_shapes, moved_shape, *operands):
    vmem = pl.BlockSpec(memory_space=pltpu.VMEM)
    single = len(out_shapes) == 1
    shapes = [jax.ShapeDtypeStruct(shape, jnp.float32) for shape in out_shapes]
    order = moved_shape[1]
    return pl.pallas_call(
        kernel,
        out_shape=shapes[0] if single else shapes,
        in_specs=[vmem] * len(operands),
        out_specs=vmem if single else [vmem] * len(shapes),
        scratch_shapes=[
            pltpu.VMEM((order, order), jnp.float32),
            pltpu.VMEM(moved_shape, jnp.float32),
            pltpu.VMEM((BLOCK, BLOCK), jnp.float32),
            pltpu.VMEM((BLOCK, BLOCK), jnp.float32),
        ],
        compiler_params=pltpu.CompilerParams(vmem_limit_bytes=32 * 2**20),
        cost_estimate=pl.CostEstimate(
            flops=160 * moved_shape[0] * order * order,
            bytes_accessed=4 * moved_shape[0] * order,
            transcendentals=0,
        ),
    )(*operands)


def whiten(gram_matrix, rows, scale):
    kernel = functools.partial(whiten_kernel, scale)
    return solve_call(kernel, [rows.shape], rows.shape, gram_matrix, rows)


def whiten_first(gram_matrix, rows):
    count, order = rows.shape
    return solve_call(
        first_kernel, [rows.shape, (order, order)], (count + order, order), gram_matrix, rows
    )


def whiten_second(gram_rows, rows, done, solve, scale):
    count, order = rows.shape
    kernel = functools.partial(second_kernel, scale)
    return solve_call(
        kernel, [(count, 2 * order)], rows.shape, gram_rows, rows, done, solve
    )


def own_gram(rows):
    return lax.dot_general(rows, rows, (((0,), (0,)), ((), ())), precision=HIGHEST)


def general_body(data, landmarks, basis):
    exponent_scale = math.sqrt(data.shape[1])
    all_marks = landmarks.shape[0] * lax.axis_size("blk")
    total_rows = data.shape[0] * lax.axis_size("blk") * lax.axis_size("dp")
    tile = kernel_tile(
        unit_rows(data),
        lax.all_gather(unit_rows(landmarks), "blk", axis=0, tiled=True),
        exponent_scale,
    )
    projected = jnp.dot(
        tile, lax.all_gather(basis, "blk", axis=0, tiled=True), preferred_element_type=jnp.float32
    )
    column_sums = lax.psum(lax.psum(jnp.sum(projected, axis=0), "blk"), "dp")
    centred = (projected - column_sums / total_rows).astype(jnp.bfloat16)
    partial = lax.dot_general(
        tile, centred, (((0,), (0,)), ((), ())), preferred_element_type=jnp.float32
    )
    panel = lax.psum_scatter(partial, "blk", scatter_dimension=0, tiled=True)
    shares = lax.psum_scatter(panel, "dp", scatter_dimension=0, tiled=True)
    gram_matrix = lax.psum(own_gram(shares), ("blk", "dp"))
    local_rows = whiten(gram_matrix, shares, math.sqrt(all_marks))
    return lax.all_gather(local_rows, "dp", axis=0, tiled=True)


def tile_kernel(exponent_scale, split, data_ref, odd_ref, *refs):
    half_refs, other_refs = refs[:split], refs[split:-3]
    tile_ref, stats_ref, unit_ref = refs[-3:]
    at = 0
    if other_refs:
        odd = odd_ref[0] == 1
        for half_ref, other_ref in zip(half_refs, other_refs):
            count, width = half_ref.shape
            here = slice(at, at + count)
            for low in (True, False):
                span = slice(0, width) if low else slice(width, 2 * width)

                @pl.when(odd == low)
                def _():
                    unit_ref[here, span] = other_ref[...]

                @pl.when(odd != low)
                def _():
                    unit_ref[here, span] = half_ref[...]

            at += count
        unit_ref[...] = unit_rows(unit_ref[...])
    else:
        unit_ref[...] = unit_rows(half_refs[0][...])
    rows = data_ref.shape[0]
    step = math.gcd(rows, 480)

    def add_rows(index, stats):
        here = pl.ds(pl.multiple_of(index * step, step), step)
        scores = lax.dot_general(
            data_ref[here, :],
            unit_ref[...],
            (((1,), (1,)), ((), ())),
            preferred_element_type=jnp.float32,
        )
        tile = jnp.exp(exponent_scale * scores).astype(jnp.bfloat16)
        tile_ref[here, :] = tile
        wide = tile.astype(jnp.float32)
        return stats[0] + jnp.sum(wide, axis=0, keepdims=True), stats[1] + jnp.sum(
            wide * wide, axis=0, keepdims=True
        )

    none = jnp.zeros((1, unit_ref.shape[0]), jnp.float32)
    stats_ref[...] = jnp.concatenate(lax.fori_loop(0, rows // step, add_rows, (none, none), unroll=2), 0)


def tile_call(unit_data, odd, halves, others, exponent_scale):
    vmem = pl.BlockSpec(memory_space=pltpu.VMEM)
    rows, depth = unit_data.shape
    count = sum(half.shape[0] for half in halves)
    return pl.pallas_call(
        functools.partial(tile_kernel, exponent_scale, len(halves)),
        out_shape=[
            jax.ShapeDtypeStruct((rows, count), jnp.bfloat16),
            jax.ShapeDtypeStruct((2, count), jnp.float32),
        ],
        in_specs=[vmem, pl.BlockSpec(memory_space=pltpu.SMEM)] + [vmem] * (len(halves) + len(others)),
        out_specs=[vmem, vmem],
        scratch_shapes=[pltpu.VMEM((count, depth), jnp.bfloat16)],
        compiler_params=pltpu.CompilerParams(vmem_limit_bytes=32 * 2**20),
        cost_estimate=pl.CostEstimate(
            flops=2 * rows * count * depth,
            bytes_accessed=2 * rows * (count + depth),
            transcendentals=rows * count,
        ),
    )(unit_data, odd, *halves, *others)


def over_cores(values):
    return lax.ppermute(values, "blk", SWAP_CORE)


def over_y(values):
    return lax.ppermute(values, "blk", SWAP_Y)


def after(values, *others):
    return lax.optimization_barrier((values, *others))[0]


def product_of(left, right):
    return lax.dot_general(left, right, (((0,), (0,)), ((), ())), precision=HIGHEST)


def product(left, right):
    return jnp.dot(left, right, preferred_element_type=jnp.float32)


def weigh_kernel(stats_ref, near_ref, first_ref, last_ref, out_ref):
    count, width = first_ref.shape

    def split(weights):
        top = weights.astype(jnp.bfloat16).astype(jnp.float32)
        middle = (weights - top).astype(jnp.bfloat16).astype(jnp.float32)
        low = weights - top - middle
        row = lax.broadcasted_iota(jnp.int32, (8, count), 0)
        parts = jnp.where(row == 0, top, jnp.where(row == 1, middle, jnp.where(row == 2, low, 0.0)))
        return parts.astype(jnp.bfloat16)

    near, far = split(stats_ref[:1, :count]), split(stats_ref[:1, count:])
    for index, far_ref in enumerate((first_ref, last_ref)):
        span = slice(index * width, (index + 1) * width)
        near_rows, far_rows = near_ref[:, span], far_ref[...]
        value = jnp.sum(product(near, near_rows), axis=0, keepdims=True) + jnp.sum(
            product(far, far_rows), axis=0, keepdims=True
        )
        size = product(near, jnp.abs(near_rows)) + product(far, jnp.abs(far_rows))
        out_ref[:, span] = jnp.concatenate([value, size[:1]], 0)


def weigh_call(stats, near_rows, first_rows, last_rows):
    return pl.pallas_call(
        weigh_kernel,
        out_shape=jax.ShapeDtypeStruct((2, near_rows.shape[1]), jnp.float32),
        in_specs=[pl.BlockSpec(memory_space=pltpu.VMEM)] * 4,
        out_specs=pl.BlockSpec(memory_space=pltpu.VMEM),
        compiler_params=pltpu.CompilerParams(vmem_limit_bytes=16 * 2**20),
    )(stats, near_rows, first_rows, last_rows)


def as_half(values):
    return lax.optimization_barrier(values.astype(jnp.float16))


def body(data, landmarks, basis):
    exponent_scale = math.sqrt(data.shape[1])
    all_marks = landmarks.shape[0] * lax.axis_size("blk")
    total_rows = data.shape[0] * lax.axis_size("blk") * lax.axis_size("dp")
    second = lax.axis_index("blk") % 2 == 1
    place = lax.axis_index("dp")
    odd = place % 2 == 1
    inner = (place == 1) | (place == 2)
    marks = landmarks.shape[0]
    half_marks = marks // 2
    width = basis.shape[1] // 2

    previous = []

    def ordered(step, operand, *others):
        if previous:
            operand = lax.optimization_barrier((operand, previous.pop()))[0]
        value = step(operand, *others)
        previous.append(jax.tree.leaves(value)[0])
        return value

    def own_half(values):
        middle = values.shape[1] // 2
        return jnp.where(odd, values[:, middle:], values[:, :middle])

    def over_near(values):
        return lax.ppermute(values, "dp", SWAP_NEAR)

    basis_parts = [basis[:, :width], basis[:, width:]]
    near_marks = [landmarks[:half_marks], landmarks[half_marks:]]
    first_half = own_half(near_marks[0])
    received = [over_y(first_half)]
    other_data = over_cores(data)
    second_half = own_half(after(near_marks[1], other_data, first_half))
    received.append(over_y(second_half))
    unit_data = unit_rows(jnp.concatenate([after(data, second_half), other_data], 0))
    parity = (place % 2).astype(jnp.int32).reshape(1)
    tiles, tile_stats = [], []

    def add_tile(halves, others=()):
        tile, stats = ordered(
            lambda first: tile_call(unit_data, parity, [first, *halves[1:]], others, exponent_scale),
            halves[0],
        )
        tiles.append(tile)
        tile_stats.append(stats)

    def arrived(values):
        return ordered(lambda value: value, values)

    def mark_arrived(index):
        mark_halves.append(arrived(received[index]))
        mark_others.append(over_near(mark_halves[index]))

    mark_halves, mark_others = [], []
    add_tile([landmarks])
    far_basis = [over_y(after(basis_parts[0], tiles[0]))]
    mark_arrived(0)
    near_parts = [ordered(product, tiles[0], part) for part in basis_parts]
    far_basis.append(over_y(after(basis_parts[1], *near_parts)))
    mark_arrived(1)
    add_tile(mark_halves[:1], mark_others[:1])
    far_basis[0] = arrived(far_basis[0])
    add_tile(mark_halves[1:], mark_others[1:])
    near_tiles = [tiles[0][:, :half_marks], tiles[0][:, half_marks:]]
    far_tiles = tiles[1:]
    stats = jnp.concatenate(tile_stats, 1)
    near, far, across = (lax.ppermute(stats, "dp", swap) for swap in (SWAP_NEAR, SWAP_FAR, ACROSS))
    stats = ordered(lambda *four: (four[0] + four[1]) + (four[2] + four[3]), stats, near, far, across)
    far_basis[1] = arrived(far_basis[1])
    stats = after(stats, far_basis[1])
    stats = stats + over_y(jnp.concatenate([stats[:, marks:], stats[:, :marks]], 1))
    peaks = jnp.sqrt(stats[1:]).reshape(4, half_marks, 1)
    weighed = weigh_call(stats, basis, *far_basis)
    weighed = weighed + over_cores(weighed)
    means = weighed[:1] / total_rows
    scales = 2.0**14 / (1.02 * jnp.maximum(weighed[1:], 1e-30))

    def project(far_rows, near_part):
        return (
            near_part
            + product(far_tiles[0], far_rows[:half_marks])
            + product(far_tiles[1], far_rows[half_marks:])
        )

    def centre(other, part, columns):
        rows = data.shape[0]
        projected = part + jnp.concatenate([other[rows:], other[:rows]], 0)
        return (projected - means[:, columns]).astype(jnp.bfloat16), scales[:, columns]

    def part_of(tile, peak, pair):
        centred, scale = pair
        part = lax.dot_general(
            tile, centred, (((0,), (0,)), ((), ())), preferred_element_type=jnp.float32
        )
        return part * (scale * (1.0 / peak))

    def send_step(tile, index, pair):
        return as_half(part_of(tile, peaks[2 + index], pair))

    def panel_step(received, index, pair):
        return as_half(part_of(near_tiles[index], peaks[index], pair) + received.astype(jnp.float32))

    def sum_step(received, kept):
        return as_half(kept.astype(jnp.float32) + received.astype(jnp.float32))

    def final_step(given, total, index):
        chosen = jnp.where(inner, total, given).astype(jnp.float32)
        return chosen * (peaks[index] * 2.0**-14)

    def split_step(part):
        middle = part.shape[0] // 2
        top, bottom = part[:middle], part[middle:]
        return jnp.where(second, bottom, top), jnp.where(second, top, bottom)

    def add_step(received, kept):
        return received + kept

    def gather_step(others, kept):
        return jnp.concatenate(
            [jnp.where(second, others, kept), jnp.where(second, kept, others)], 0
        )

    spans = [slice(0, width), slice(width, 2 * width)]
    first_part = project(far_basis[0], near_parts[0])
    last_part = project(far_basis[1], near_parts[1])
    last_other = over_cores(after(last_part, means))
    centred = [ordered(centre, over_cores(first_part), first_part, spans[0])]
    chunks = [(0, centred[0]), (1, centred[0])]
    received = [None] * 4

    def send(i):
        index, pair = chunks[i]
        received[i] = over_y(ordered(send_step, far_tiles[index], index, pair))

    panels, outers, pairs, crosses, totals, givens, finals = ([None] * 4 for _ in range(7))

    def panel(i):
        panels[i] = ordered(panel_step, received[i], *chunks[i])
        outers[i] = lax.ppermute(panels[i], "dp", TO_INNER)

    def joint(i):
        pairs[i] = ordered(sum_step, outers[i], panels[i])
        crosses[i] = lax.ppermute(pairs[i], "dp", SWAP_INNER)

    def total(i):
        totals[i] = ordered(sum_step, crosses[i], pairs[i])
        givens[i] = lax.ppermute(totals[i], "dp", TO_OUTER)

    def final(i):
        finals[i] = ordered(final_step, givens[i], totals[i], chunks[i][0])

    send(0)
    send(1)
    centred.append(ordered(centre, last_other, last_part, spans[1]))
    chunks += [(0, centred[1]), (1, centred[1])]
    panel(0)
    send(2)
    panel(1)
    send(3)
    joint(0)
    panel(2)
    joint(1)
    total(0)
    panel(3)
    joint(2)
    total(1)
    joint(3)
    total(2)
    final(0)
    final(1)
    first = jnp.concatenate(finals[:2], 0)
    kept, sent = split_step(ordered(product_of, first, first))
    arriving = over_cores(sent)
    total(3)
    kept = ordered(add_step, arriving, kept)
    arriving = over_y(kept)
    final(2)
    kept = ordered(add_step, arriving, kept)
    arriving = over_cores(kept)
    final(3)
    last = jnp.concatenate(finals[2:], 0)
    last_kept, last_sent = split_step(product_of(last, jnp.concatenate([first, last], 1)))
    last_kept = last_kept + over_cores(last_sent)
    last_arriving = over_y(last_kept)
    first_gram = gather_step(after(arriving, last_kept), kept)
    done, solve = whiten_first(first_gram, first)
    last_arriving = after(last_arriving, done)
    last_kept = last_kept + last_arriving
    last_gram = gather_step(over_cores(last_kept), last_kept)
    return whiten_second(last_gram, last, done, solve, math.sqrt(all_marks))


def solution(mesh):
    in_specs = (
        P(("groups", "blk", "dp"), None),
        P(("groups", "blk"), None),
        P(("groups", "blk"), None),
    )
    out_specs = P(("groups", "blk"), None)
    fits = mesh.shape["blk"] == 4 and mesh.shape["dp"] == 4
    return jax.shard_map(
        body if fits else general_body,
        mesh=mesh,
        in_specs=in_specs,
        out_specs=out_specs,
        check_vma=False,
    )
```

profile of v0, /device:TPU:0, one launch (start us, length us, event | category | flops | bytes accessed | tf_op | source)
XLA Modules:
  0.0 146.4 jit_solution(11560163679947780230)
XLA Ops:
  1.6 2.7 %collective-permute-start.1 = (bf16[512,384]{1,0:T(8,128)(2,1)S(1)}, bf16[512,384]{1,0:T(8,128)(2,1)S(1)}, u32[]{:S(2)}, u32[]{:S(2)}) collective-permute-start(bf16[512,384]{1,0:T(8,128)(2,1)S(1)} %slice_select_fusion.1), channel_id=1, source_target_pairs={{0,8},{8,0},{4,12},{12,4},{1,9},{9,1},{5,13},{13,5},{2,10},{10,2},... | collective-permute-start | bytes 1179656 | tf_op jit(solution)/shard_map/ppermute | solution.py:325
  4.5 2.2 %collective-permute-start.2 = (bf16[512,384]{1,0:T(8,128)(2,1)S(1)}, bf16[512,384]{1,0:T(8,128)(2,1)S(1)}, u32[]{:S(2)}, u32[]{:S(2)}) collective-permute-start(bf16[512,384]{1,0:T(8,128)(2,1)S(1)} %slice_select_fusion), channel_id=1, source_target_pairs={{0,8},{8,0},{4,12},{12,4},{1,9},{9,1},{5,13},{13,5},{2,10},{10,2},... | collective-permute-start | bytes 1179656 | tf_op jit(solution)/shard_map/ppermute | solution.py:325
  6.7 2.0 %fusion = f32[1920]{0:T(1024)S(1)} fusion(bf16[960,768]{1,0:T(8,128)(2,1)} %collective-permute-done, bf16[960,768]{1,0:T(8,128)(2,1)S(1)} %copy-done.2), kind=kLoop, calls=%fused_computation.2 | loop fusion | flops 8845440 | bytes 2956800 | tf_op jit(solution)/shard_map/reduce_sum | solution.py:27
  8.7 2.5 %fusion.1.data_ref = bf16[1920,768]{1,0:T(8,128)(2,1)S(1)} fusion(f32[1920]{0:T(1024)S(1)} %add_rsqrt_fusion, bf16[960,768]{1,0:T(8,128)(2,1)} %collective-permute-done, bf16[960,768]{1,0:T(8,128)(2,1)S(1)} %copy-done.2), kind=kLoop, calls=%fused_computation.3 | loop fusion | flops 8847360 | bytes 5905920 | tf_op jit(solution)/shard_map/convert_element_type | solution.py:27
  11.3 4.9 %shard_map.37 = (bf16[1920,1024]{1,0:T(8,128)(2,1)S(1)}, f32[2,1024]{1,0:T(2,128)S(1)}) custom-call(bf16[1920,768]{1,0:T(8,128)(2,1)S(1)} %fusion.1.data_ref, s32[1]{0:T(128)} %bitcast.odd_ref, bf16[1024,768]{1,0:T(8,128)(2,1)S(1)} %copy-done.1), custom_call_target="tpu_custom_call" | custom-call | flops 3019898880 | bytes 6881280 | tf_op jit(solution)/shard_map/pallas_call | solution.py:302
  16.1 1.6 %collective-permute-start.3 = (bf16[512,384]{1,0:T(8,128)(2,1)S(1)}, bf16[512,384]{1,0:T(8,128)(2,1)S(1)}, u32[]{:S(2)}, u32[]{:S(2)}) collective-permute-start(bf16[512,384]{1,0:T(8,128)(2,1)S(1)} %collective-permute-done.1.refs_0_), channel_id=1, source_target_pairs={{0,1},{1,0},{2,3},{3,2},{4,5},{5,4},{6,7},{7,6},{8,9},{9,8},{10,11... | collective-permute-start | bytes 1179656 | tf_op jit(solution)/shard_map/ppermute | solution.py:402
  20.8 1.6 %collective-permute-start.4 = (bf16[1024,256]{1,0:T(8,128)(2,1)S(1)}, bf16[1024,256]{1,0:T(8,128)(2,1)S(1)}, u32[]{:S(2)}, u32[]{:S(2)}) collective-permute-start(bf16[1024,256]{1,0:T(8,128)(2,1)S(1)} %get-tuple-element.64), channel_id=1, source_target_pairs={{0,8},{8,0},{4,12},{12,4},{1,9},{9,1},{5,13},{13,5},{2,10},{10,2},... | collective-permute-start | bytes 1572872 | tf_op jit(solution)/shard_map/ppermute | solution.py:325
  22.7 2.0 %collective-permute-start.6 = (bf16[512,384]{1,0:T(8,128)(2,1)S(1)}, bf16[512,384]{1,0:T(8,128)(2,1)S(1)}, u32[]{:S(2)}, u32[]{:S(2)}) collective-permute-start(bf16[512,384]{1,0:T(8,128)(2,1)S(1)} %collective-permute-done.2.refs_0_), channel_id=1, source_target_pairs={{0,1},{1,0},{2,3},{3,2},{4,5},{5,4},{6,7},{7,6},{8,9},{9,8},{10,11... | collective-permute-start | bytes 1179656 | tf_op jit(solution)/shard_map/ppermute | solution.py:402
  24.7 3.5 %collective-permute-done.3.refs_1_ = bf16[512,384]{1,0:T(8,128)(2,1)S(1)} collective-permute-done((bf16[512,384]{1,0:T(8,128)(2,1)S(1)}, bf16[512,384]{1,0:T(8,128)(2,1)S(1)}, u32[]{:S(2)}, u32[]{:S(2)}) %collective-permute-start.3) | collective-permute-done | bytes 393248 | tf_op jit(solution)/shard_map/ppermute | solution.py:402
  28.2 2.7 %shard_map.38 = (bf16[1920,512]{1,0:T(8,128)(2,1)S(1)}, f32[2,512]{1,0:T(2,128)S(1)}) custom-call(bf16[1920,768]{1,0:T(8,128)(2,1)S(1)} %fusion.1.data_ref, s32[1]{0:T(128)} %bitcast.odd_ref, bf16[512,384]{1,0:T(8,128)(2,1)S(1)} %collective-permute-done.1.refs_0_, bf16[512,384]{1,0:T(8,128)(2,1)S(1)} %collective-permute-done.3.refs_1_), custom_call_target="tpu_custom_call" | custom-call | flops 1509949440 | bytes 4915200 | tf_op jit(solution)/shard_map/pallas_call | solution.py:302
  30.9 3.0 %collective-permute-done.5.first_ref = bf16[1024,256]{1,0:T(8,128)(2,1)S(1)} collective-permute-done((bf16[1024,256]{1,0:T(8,128)(2,1)S(1)}, bf16[1024,256]{1,0:T(8,128)(2,1)S(1)}, u32[]{:S(2)}, u32[]{:S(2)}) %collective-permute-start.5) | collective-permute-done | bytes 524320 | tf_op jit(solution)/shard_map/ppermute | solution.py:325
  35.5 2.9 %shard_map.39 = (bf16[1920,512]{1,0:T(8,128)(2,1)S(1)}, f32[2,512]{1,0:T(2,128)S(1)}) custom-call(bf16[1920,768]{1,0:T(8,128)(2,1)S(1)} %fusion.1.data_ref, s32[1]{0:T(128)} %bitcast.odd_ref, bf16[512,384]{1,0:T(8,128)(2,1)S(1)} %collective-permute-done.2.refs_0_, bf16[512,384]{1,0:T(8,128)(2,1)S(1)} %collective-permute-done.6.refs_1_), custom_call_target="tpu_custom_call" | custom-call | flops 1509949440 | bytes 4915200 | tf_op jit(solution)/shard_map/pallas_call | solution.py:302
  38.4 1.7 %collective-permute-start.7 = (f32[2,2048]{1,0:T(2,128)S(1)}, f32[2,2048]{1,0:T(2,128)S(1)}, u32[]{:S(2)}, u32[]{:S(2)}) collective-permute-start(f32[2,2048]{1,0:T(2,128)S(1)} %constant_dynamic-update-slice_fusion), channel_id=1, source_target_pairs={{0,1},{1,0},{2,3},{3,2},{4,5},{5,4},{6,7},{7,6},{8,9},{9,8},{10,11... | collective-permute-start | bytes 49160 | tf_op jit(solution)/shard_map/ppermute | solution.py:443
  40.1 2.6 %collective-permute-start.8 = (f32[2,2048]{1,0:T(2,128)S(1)}, f32[2,2048]{1,0:T(2,128)S(1)}, u32[]{:S(2)}, u32[]{:S(2)}) collective-permute-start(f32[2,2048]{1,0:T(2,128)S(1)} %constant_dynamic-update-slice_fusion), channel_id=1, source_target_pairs={{0,2},{2,0},{1,3},{3,1},{4,6},{6,4},{5,7},{7,5},{8,10},{10,8},{9,1... | collective-permute-start | bytes 49160 | tf_op jit(solution)/shard_map/ppermute | solution.py:443
  44.8 3.4 %collective-permute-done.9 = f32[2,2048]{1,0:T(2,128)S(1)} collective-permute-done((f32[2,2048]{1,0:T(2,128)S(1)}, f32[2,2048]{1,0:T(2,128)S(1)}, u32[]{:S(2)}, u32[]{:S(2)}) %collective-permute-start.9) | collective-permute-done | bytes 16416 | tf_op jit(solution)/shard_map/ppermute | solution.py:443
  50.1 1.9 %collective-permute-done.10 = f32[2,2048]{1,0:T(2,128)S(1)} collective-permute-done((f32[2,2048]{1,0:T(2,128)S(1)}, f32[2,2048]{1,0:T(2,128)S(1)}, u32[]{:S(2)}, u32[]{:S(2)}) %collective-permute-start.10) | collective-permute-done | bytes 16416 | tf_op jit(solution)/shard_map/ppermute | solution.py:325
  59.1 5.8 %collective-permute-done.14 = f16[512,256]{1,0:T(8,128)(2,1)S(1)} collective-permute-done((f16[512,256]{1,0:T(8,128)(2,1)S(1)}, f16[512,256]{1,0:T(8,128)(2,1)S(1)}, u32[]{:S(2)}, u32[]{:S(2)}) %collective-permute-start.14) | collective-permute-done | bytes 262176 | tf_op jit(solution)/shard_map/ppermute | solution.py:325
  68.9 1.5 %collective-permute-done.17 = f16[512,256]{1,0:T(8,128)(2,1)S(1)} collective-permute-done((f16[512,256]{1,0:T(8,128)(2,1)S(1)}, f16[512,256]{1,0:T(8,128)(2,1)S(1)}, u32[]{:S(2)}, u32[]{:S(2)}) %collective-permute-start.17) | collective-permute-done | bytes 262176 | tf_op jit(solution)/shard_map/ppermute | solution.py:325
  76.8 2.8 %collective-permute-start.18 = (f16[512,256]{1,0:T(8,128)(2,1)S(1)}, f16[512,256]{1,0:T(8,128)(2,1)S(1)}, u32[]{:S(2)}, u32[]{:S(2)}) collective-permute-start(f16[512,256]{1,0:T(8,128)(2,1)S(1)} %fusion.55), channel_id=1, source_target_pairs={{0,1},{3,2},{4,5},{7,6},{8,9},{11,10},{12,13},{15,14},{16,17},{19,... | collective-permute-start | bytes 786440 | tf_op jit(solution)/shard_map/ppermute | solution.py:515
  80.5 1.5 %collective-permute-start.26 = (f16[512,256]{1,0:T(8,128)(2,1)S(1)}, f16[512,256]{1,0:T(8,128)(2,1)S(1)}, u32[]{:S(2)}, u32[]{:S(2)}) collective-permute-start(f16[512,256]{1,0:T(8,128)(2,1)S(1)} %add_convert_fusion.5), channel_id=1, source_target_pairs={{1,0},{2,3},{5,4},{6,7},{9,8},{10,11},{13,12},{14,15},{17,16},{18,... | collective-permute-start | bytes 786440 | tf_op jit(solution)/shard_map/ppermute | solution.py:523
  82.8 4.6 %collective-permute-start.23 = (f16[512,256]{1,0:T(8,128)(2,1)S(1)}, f16[512,256]{1,0:T(8,128)(2,1)S(1)}, u32[]{:S(2)}, u32[]{:S(2)}) collective-permute-start(f16[512,256]{1,0:T(8,128)(2,1)S(1)} %fusion.46), channel_id=1, source_target_pairs={{0,1},{3,2},{4,5},{7,6},{8,9},{11,10},{12,13},{15,14},{16,17},{19,... | collective-permute-start | bytes 786440 | tf_op jit(solution)/shard_map/ppermute | solution.py:515
  89.6 1.7 %collective-permute-done.23 = f16[512,256]{1,0:T(8,128)(2,1)S(1)} collective-permute-done((f16[512,256]{1,0:T(8,128)(2,1)S(1)}, f16[512,256]{1,0:T(8,128)(2,1)S(1)}, u32[]{:S(2)}, u32[]{:S(2)}) %collective-permute-start.23) | collective-permute-done | bytes 262176 | tf_op jit(solution)/shard_map/ppermute | solution.py:515
  93.6 3.7 %collective-permute-done.27 = f16[512,256]{1,0:T(8,128)(2,1)S(1)} collective-permute-done((f16[512,256]{1,0:T(8,128)(2,1)S(1)}, f16[512,256]{1,0:T(8,128)(2,1)S(1)}, u32[]{:S(2)}, u32[]{:S(2)}) %collective-permute-start.27) | collective-permute-done | bytes 262176 | tf_op jit(solution)/shard_map/ppermute | solution.py:523
  97.6 1.8 %fusion.73 = f32[256,256]{1,0:T(8,128)S(1)} fusion(f32[1024,256]{1,0:T(8,128)S(1)} %pad_maximum_fusion.1.rows_ref, f32[512,256]{1,0:T(8,128)S(1)} %convert_multiply_fusion.4, f32[512,256]{1,0:T(8,128)S(1)} %convert_multiply_fusion.5), kind=kOutput, calls=%fused_computation.103 | convolution fusion | flops 805568512 | bytes 2359296 | tf_op jit(solution)/shard_map/dot_general | solution.py:333
  101.0 1.8 %collective-permute-start.31 = (f32[128,256]{1,0:T(8,128)S(1)}, f32[128,256]{1,0:T(8,128)S(1)}, u32[]{:S(2)}, u32[]{:S(2)}) collective-permute-start(f32[128,256]{1,0:T(8,128)S(1)} %select_add_fusion.1), channel_id=1, source_target_pairs={{0,8},{8,0},{4,12},{12,4},{1,9},{9,1},{5,13},{13,5},{2,10},{10,2},... | collective-permute-start | bytes 393224 | tf_op jit(solution)/shard_map/ppermute | solution.py:325
  103.2 3.8 %collective-permute-done.31 = f32[128,256]{1,0:T(8,128)S(1)} collective-permute-done((f32[128,256]{1,0:T(8,128)S(1)}, f32[128,256]{1,0:T(8,128)S(1)}, u32[]{:S(2)}, u32[]{:S(2)}) %collective-permute-start.31) | collective-permute-done | bytes 131104 | tf_op jit(solution)/shard_map/ppermute | solution.py:325
  107.0 3.3 %collective-permute-done.30 = f16[512,256]{1,0:T(8,128)(2,1)S(1)} collective-permute-done((f16[512,256]{1,0:T(8,128)(2,1)S(1)}, f16[512,256]{1,0:T(8,128)(2,1)S(1)}, u32[]{:S(2)}, u32[]{:S(2)}) %collective-permute-start.30) | collective-permute-done | bytes 262176 | tf_op jit(solution)/shard_map/ppermute | solution.py:523
  110.4 2.0 %fusion.2 = f32[256,512]{1,0:T(8,128)S(1)} fusion(f32[512,256]{1,0:T(8,128)S(1)} %convert_multiply_fusion.2, f32[512,256]{1,0:T(8,128)S(1)} %convert_multiply_fusion.3, f32[512,256]{1,0:T(8,128)S(1)} %convert_multiply_fusion.4, f32[512,256]{1,0:T(8,128)S(1)} %convert_multiply_fusion.5), kind=kOutput, calls=%fused_computation.9 | convolution fusion | flops 1612447744 | bytes 2621440 | tf_op jit(solution)/shard_map/dot_general | solution.py:333
  114.0 1.8 %collective-permute-start.33 = (f32[128,512]{1,0:T(8,128)S(1)}, f32[128,512]{1,0:T(8,128)S(1)}, u32[]{:S(2)}, u32[]{:S(2)}) collective-permute-start(f32[128,512]{1,0:T(8,128)S(1)} %select_add_fusion), channel_id=1, source_target_pairs={{0,8},{8,0},{4,12},{12,4},{1,9},{9,1},{5,13},{13,5},{2,10},{10,2},... | collective-permute-start | bytes 786440 | tf_op jit(solution)/shard_map/ppermute | solution.py:325
  115.9 13.2 %shard_map.41 = (f32[1024,256]{1,0:T(8,128)S(1)}, f32[256,256]{1,0:T(8,128)S(1)}) custom-call(f32[256,256]{1,0:T(8,128)S(1)} %pad_maximum_fusion.5.gram_ref, f32[1024,256]{1,0:T(8,128)S(1)} %pad_maximum_fusion.1.rows_ref), custom_call_target="tpu_custom_call" | custom-call | flops 13421772800 | bytes 1310720 | tf_op jit(solution)/shard_map/pallas_call | solution.py:184
  129.3 1.4 collective-permute-done.35
  130.9 15.6 %shard_map.42 = f32[1024,512]{1,0:T(8,128)} custom-call(f32[256,512]{1,0:T(8,128)S(1)} %pad_maximum_fusion.3.gram_ref, f32[1024,256]{1,0:T(8,128)S(1)} %pad_maximum_fusion.2.rows_ref, f32[1024,256]{1,0:T(8,128)S(1)} %get-tuple-element.102.done_ref, f32[256,256]{1,0:T(8,128)S(1)} %get-tuple-element.104.solve_ref), custom_call_target="tpu_custom_call" | custom-call | flops 10737418240 | bytes 1048576 | tf_op jit(solution)/shard_map/pallas_call | solution.py:184
  (116 shorter events, 38.3 us)
Async XLA Ops:
  0.0 4.4 %collective-permute-start = (bf16[960,768]{1,0:T(8,128)(2,1)}, bf16[960,768]{1,0:T(8,128)(2,1)}, u32[]{:S(2)}, u32[]{:S(2)}) collective-permute-start(bf16[960,768]{1,0:T(8,128)(2,1)} %param.3), channel_id=1, source_target_pairs={{0,4},{4,0},{8,12},{12,8},{1,5},{5,1},{9,13},{13,9},{2,6},{6,2},{1... | collective-permute-start | bytes 4423688 | tf_op jit(solution)/shard_map/ppermute | solution.py:321
  1.6 14.5 %collective-permute-start.1 = (bf16[512,384]{1,0:T(8,128)(2,1)S(1)}, bf16[512,384]{1,0:T(8,128)(2,1)S(1)}, u32[]{:S(2)}, u32[]{:S(2)}) collective-permute-start(bf16[512,384]{1,0:T(8,128)(2,1)S(1)} %slice_select_fusion.1), channel_id=1, source_target_pairs={{0,8},{8,0},{4,12},{12,4},{1,9},{9,1},{5,13},{13,5},{2,10},{10,2},... | collective-permute-start | bytes 1179656 | tf_op jit(solution)/shard_map/ppermute | solution.py:325
  4.5 18.2 %collective-permute-start.2 = (bf16[512,384]{1,0:T(8,128)(2,1)S(1)}, bf16[512,384]{1,0:T(8,128)(2,1)S(1)}, u32[]{:S(2)}, u32[]{:S(2)}) collective-permute-start(bf16[512,384]{1,0:T(8,128)(2,1)S(1)} %slice_select_fusion), channel_id=1, source_target_pairs={{0,8},{8,0},{4,12},{12,4},{1,9},{9,1},{5,13},{13,5},{2,10},{10,2},... | collective-permute-start | bytes 1179656 | tf_op jit(solution)/shard_map/ppermute | solution.py:325
  16.1 12.1 %collective-permute-start.3 = (bf16[512,384]{1,0:T(8,128)(2,1)S(1)}, bf16[512,384]{1,0:T(8,128)(2,1)S(1)}, u32[]{:S(2)}, u32[]{:S(2)}) collective-permute-start(bf16[512,384]{1,0:T(8,128)(2,1)S(1)} %collective-permute-done.1.refs_0_), channel_id=1, source_target_pairs={{0,1},{1,0},{2,3},{3,2},{4,5},{5,4},{6,7},{7,6},{8,9},{9,8},{10,11... | collective-permute-start | bytes 1179656 | tf_op jit(solution)/shard_map/ppermute | solution.py:402
  19.0 14.9 %collective-permute-start.5 = (bf16[1024,256]{1,0:T(8,128)(2,1)S(1)}, bf16[1024,256]{1,0:T(8,128)(2,1)S(1)}, u32[]{:S(2)}, u32[]{:S(2)}) collective-permute-start(bf16[1024,256]{1,0:T(8,128)(2,1)S(1)} %get-tuple-element.67), channel_id=1, source_target_pairs={{0,8},{8,0},{4,12},{12,4},{1,9},{9,1},{5,13},{13,5},{2,10},{10,2},... | collective-permute-start | bytes 1572872 | tf_op jit(solution)/shard_map/ppermute | solution.py:325
  20.8 27.4 %collective-permute-start.4 = (bf16[1024,256]{1,0:T(8,128)(2,1)S(1)}, bf16[1024,256]{1,0:T(8,128)(2,1)S(1)}, u32[]{:S(2)}, u32[]{:S(2)}) collective-permute-start(bf16[1024,256]{1,0:T(8,128)(2,1)S(1)} %get-tuple-element.64), channel_id=1, source_target_pairs={{0,8},{8,0},{4,12},{12,4},{1,9},{9,1},{5,13},{13,5},{2,10},{10,2},... | collective-permute-start | bytes 1572872 | tf_op jit(solution)/shard_map/ppermute | solution.py:325
  22.7 12.8 %collective-permute-start.6 = (bf16[512,384]{1,0:T(8,128)(2,1)S(1)}, bf16[512,384]{1,0:T(8,128)(2,1)S(1)}, u32[]{:S(2)}, u32[]{:S(2)}) collective-permute-start(bf16[512,384]{1,0:T(8,128)(2,1)S(1)} %collective-permute-done.2.refs_0_), channel_id=1, source_target_pairs={{0,1},{1,0},{2,3},{3,2},{4,5},{5,4},{6,7},{7,6},{8,9},{9,8},{10,11... | collective-permute-start | bytes 1179656 | tf_op jit(solution)/shard_map/ppermute | solution.py:402
  38.4 5.2 %collective-permute-start.7 = (f32[2,2048]{1,0:T(2,128)S(1)}, f32[2,2048]{1,0:T(2,128)S(1)}, u32[]{:S(2)}, u32[]{:S(2)}) collective-permute-start(f32[2,2048]{1,0:T(2,128)S(1)} %constant_dynamic-update-slice_fusion), channel_id=1, source_target_pairs={{0,1},{1,0},{2,3},{3,2},{4,5},{5,4},{6,7},{7,6},{8,9},{9,8},{10,11... | collective-permute-start | bytes 49160 | tf_op jit(solution)/shard_map/ppermute | solution.py:443
  40.1 4.7 %collective-permute-start.8 = (f32[2,2048]{1,0:T(2,128)S(1)}, f32[2,2048]{1,0:T(2,128)S(1)}, u32[]{:S(2)}, u32[]{:S(2)}) collective-permute-start(f32[2,2048]{1,0:T(2,128)S(1)} %constant_dynamic-update-slice_fusion), channel_id=1, source_target_pairs={{0,2},{2,0},{1,3},{3,1},{4,6},{6,4},{5,7},{7,5},{8,10},{10,8},{9,1... | collective-permute-start | bytes 49160 | tf_op jit(solution)/shard_map/ppermute | solution.py:443
  42.6 5.5 %collective-permute-start.9 = (f32[2,2048]{1,0:T(2,128)S(1)}, f32[2,2048]{1,0:T(2,128)S(1)}, u32[]{:S(2)}, u32[]{:S(2)}) collective-permute-start(f32[2,2048]{1,0:T(2,128)S(1)} %constant_dynamic-update-slice_fusion), channel_id=1, source_target_pairs={{0,3},{3,0},{1,2},{2,1},{4,7},{7,4},{5,6},{6,5},{8,11},{11,8},{9,1... | collective-permute-start | bytes 49160 | tf_op jit(solution)/shard_map/ppermute | solution.py:443
  43.5 10.8 %collective-permute-start.13 = (f32[1920,256]{1,0:T(8,128)S(1)}, f32[1920,256]{1,0:T(8,128)S(1)}, u32[]{:S(2)}, u32[]{:S(2)}) collective-permute-start(f32[1920,256]{1,0:T(8,128)S(1)} %convolution_add_fusion), channel_id=1, source_target_pairs={{0,4},{4,0},{8,12},{12,8},{1,5},{5,1},{9,13},{13,9},{2,6},{6,2},{1... | collective-permute-start | bytes 5898248 | tf_op jit(solution)/shard_map/ppermute | solution.py:321
  48.2 3.8 %collective-permute-start.10 = (f32[2,2048]{1,0:T(2,128)S(1)}, f32[2,2048]{1,0:T(2,128)S(1)}, u32[]{:S(2)}, u32[]{:S(2)}) collective-permute-start(f32[2,2048]{1,0:T(2,128)S(1)} %pad_maximum_fusion.6), channel_id=1, source_target_pairs={{0,8},{8,0},{4,12},{12,4},{1,9},{9,1},{5,13},{13,5},{2,10},{10,2},... | collective-permute-start | bytes 49160 | tf_op jit(solution)/shard_map/ppermute | solution.py:325
  54.0 4.6 %collective-permute-start.12 = (f32[1920,256]{1,0:T(8,128)S(1)}, f32[1920,256]{1,0:T(8,128)S(1)}, u32[]{:S(2)}, u32[]{:S(2)}) collective-permute-start(f32[1920,256]{1,0:T(8,128)S(1)} %convolution_add_fusion.2), channel_id=1, source_target_pairs={{0,4},{4,0},{8,12},{12,8},{1,5},{5,1},{9,13},{13,9},{2,6},{6,2},{1... | collective-permute-start | bytes 5898248 | tf_op jit(solution)/shard_map/ppermute | solution.py:321
  55.6 9.2 %collective-permute-start.14 = (f16[512,256]{1,0:T(8,128)(2,1)S(1)}, f16[512,256]{1,0:T(8,128)(2,1)S(1)}, u32[]{:S(2)}, u32[]{:S(2)}) collective-permute-start(f16[512,256]{1,0:T(8,128)(2,1)S(1)} %fusion.58), channel_id=1, source_target_pairs={{0,8},{8,0},{4,12},{12,4},{1,9},{9,1},{5,13},{13,5},{2,10},{10,2},... | collective-permute-start | bytes 786440 | tf_op jit(solution)/shard_map/ppermute | solution.py:325
  57.6 12.8 %collective-permute-start.17 = (f16[512,256]{1,0:T(8,128)(2,1)S(1)}, f16[512,256]{1,0:T(8,128)(2,1)S(1)}, u32[]{:S(2)}, u32[]{:S(2)}) collective-permute-start(f16[512,256]{1,0:T(8,128)(2,1)S(1)} %fusion.59), channel_id=1, source_target_pairs={{0,8},{8,0},{4,12},{12,4},{1,9},{9,1},{5,13},{13,5},{2,10},{10,2},... | collective-permute-start | bytes 786440 | tf_op jit(solution)/shard_map/ppermute | solution.py:325
  65.6 8.8 %collective-permute-start.16 = (f16[512,256]{1,0:T(8,128)(2,1)S(1)}, f16[512,256]{1,0:T(8,128)(2,1)S(1)}, u32[]{:S(2)}, u32[]{:S(2)}) collective-permute-start(f16[512,256]{1,0:T(8,128)(2,1)S(1)} %fusion.52), channel_id=1, source_target_pairs={{0,1},{3,2},{4,5},{7,6},{8,9},{11,10},{12,13},{15,14},{16,17},{19,... | collective-permute-start | bytes 786440 | tf_op jit(solution)/shard_map/ppermute | solution.py:515
  67.7 8.3 %collective-permute-start.15 = (f16[512,256]{1,0:T(8,128)(2,1)S(1)}, f16[512,256]{1,0:T(8,128)(2,1)S(1)}, u32[]{:S(2)}, u32[]{:S(2)}) collective-permute-start(f16[512,256]{1,0:T(8,128)(2,1)S(1)} %fusion.60), channel_id=1, source_target_pairs={{0,8},{8,0},{4,12},{12,4},{1,9},{9,1},{5,13},{13,5},{2,10},{10,2},... | collective-permute-start | bytes 786440 | tf_op jit(solution)/shard_map/ppermute | solution.py:325
  71.1 8.5 %collective-permute-start.21 = (f16[512,256]{1,0:T(8,128)(2,1)S(1)}, f16[512,256]{1,0:T(8,128)(2,1)S(1)}, u32[]{:S(2)}, u32[]{:S(2)}) collective-permute-start(f16[512,256]{1,0:T(8,128)(2,1)S(1)} %fusion.49), channel_id=1, source_target_pairs={{0,1},{3,2},{4,5},{7,6},{8,9},{11,10},{12,13},{15,14},{16,17},{19,... | collective-permute-start | bytes 786440 | tf_op jit(solution)/shard_map/ppermute | solution.py:515
  73.2 8.8 %collective-permute-start.19 = (f16[512,256]{1,0:T(8,128)(2,1)S(1)}, f16[512,256]{1,0:T(8,128)(2,1)S(1)}, u32[]{:S(2)}, u32[]{:S(2)}) collective-permute-start(f16[512,256]{1,0:T(8,128)(2,1)S(1)} %fusion.61), channel_id=1, source_target_pairs={{0,8},{8,0},{4,12},{12,4},{1,9},{9,1},{5,13},{13,5},{2,10},{10,2},... | collective-permute-start | bytes 786440 | tf_op jit(solution)/shard_map/ppermute | solution.py:325
  74.5 5.9 %collective-permute-start.20 = (f16[512,256]{1,0:T(8,128)(2,1)S(1)}, f16[512,256]{1,0:T(8,128)(2,1)S(1)}, u32[]{:S(2)}, u32[]{:S(2)}) collective-permute-start(f16[512,256]{1,0:T(8,128)(2,1)S(1)} %add_convert_fusion.7), channel_id=1, source_target_pairs={{1,2},{2,1},{5,6},{6,5},{9,10},{10,9},{13,14},{14,13},{17,18},{18,... | collective-permute-start | bytes 786440 | tf_op jit(solution)/shard_map/ppermute | solution.py:519
  76.8 10.7 %collective-permute-start.18 = (f16[512,256]{1,0:T(8,128)(2,1)S(1)}, f16[512,256]{1,0:T(8,128)(2,1)S(1)}, u32[]{:S(2)}, u32[]{:S(2)}) collective-permute-start(f16[512,256]{1,0:T(8,128)(2,1)S(1)} %fusion.55), channel_id=1, source_target_pairs={{0,1},{3,2},{4,5},{7,6},{8,9},{11,10},{12,13},{15,14},{16,17},{19,... | collective-permute-start | bytes 786440 | tf_op jit(solution)/shard_map/ppermute | solution.py:515
  79.7 8.5 %collective-permute-start.24 = (f16[512,256]{1,0:T(8,128)(2,1)S(1)}, f16[512,256]{1,0:T(8,128)(2,1)S(1)}, u32[]{:S(2)}, u32[]{:S(2)}) collective-permute-start(f16[512,256]{1,0:T(8,128)(2,1)S(1)} %add_convert_fusion.6), channel_id=1, source_target_pairs={{1,2},{2,1},{5,6},{6,5},{9,10},{10,9},{13,14},{14,13},{17,18},{18,... | collective-permute-start | bytes 786440 | tf_op jit(solution)/shard_map/ppermute | solution.py:519
  80.5 13.0 %collective-permute-start.26 = (f16[512,256]{1,0:T(8,128)(2,1)S(1)}, f16[512,256]{1,0:T(8,128)(2,1)S(1)}, u32[]{:S(2)}, u32[]{:S(2)}) collective-permute-start(f16[512,256]{1,0:T(8,128)(2,1)S(1)} %add_convert_fusion.5), channel_id=1, source_target_pairs={{1,0},{2,3},{5,4},{6,7},{9,8},{10,11},{13,12},{14,15},{17,16},{18,... | collective-permute-start | bytes 786440 | tf_op jit(solution)/shard_map/ppermute | solution.py:523
  82.8 8.4 %collective-permute-start.23 = (f16[512,256]{1,0:T(8,128)(2,1)S(1)}, f16[512,256]{1,0:T(8,128)(2,1)S(1)}, u32[]{:S(2)}, u32[]{:S(2)}) collective-permute-start(f16[512,256]{1,0:T(8,128)(2,1)S(1)} %fusion.46), channel_id=1, source_target_pairs={{0,1},{3,2},{4,5},{7,6},{8,9},{11,10},{12,13},{15,14},{16,17},{19,... | collective-permute-start | bytes 786440 | tf_op jit(solution)/shard_map/ppermute | solution.py:515
  87.5 4.6 %collective-permute-start.22 = (f16[512,256]{1,0:T(8,128)(2,1)S(1)}, f16[512,256]{1,0:T(8,128)(2,1)S(1)}, u32[]{:S(2)}, u32[]{:S(2)}) collective-permute-start(f16[512,256]{1,0:T(8,128)(2,1)S(1)} %add_convert_fusion.4), channel_id=1, source_target_pairs={{1,2},{2,1},{5,6},{6,5},{9,10},{10,9},{13,14},{14,13},{17,18},{18,... | collective-permute-start | bytes 786440 | tf_op jit(solution)/shard_map/ppermute | solution.py:519
  88.3 9.1 %collective-permute-start.27 = (f16[512,256]{1,0:T(8,128)(2,1)S(1)}, f16[512,256]{1,0:T(8,128)(2,1)S(1)}, u32[]{:S(2)}, u32[]{:S(2)}) collective-permute-start(f16[512,256]{1,0:T(8,128)(2,1)S(1)} %add_convert_fusion.3), channel_id=1, source_target_pairs={{1,0},{2,3},{5,4},{6,7},{9,8},{10,11},{13,12},{14,15},{17,16},{18,... | collective-permute-start | bytes 786440 | tf_op jit(solution)/shard_map/ppermute | solution.py:523
  91.4 8.2 %collective-permute-start.29 = (f16[512,256]{1,0:T(8,128)(2,1)S(1)}, f16[512,256]{1,0:T(8,128)(2,1)S(1)}, u32[]{:S(2)}, u32[]{:S(2)}) collective-permute-start(f16[512,256]{1,0:T(8,128)(2,1)S(1)} %add_convert_fusion.2), channel_id=1, source_target_pairs={{1,2},{2,1},{5,6},{6,5},{9,10},{10,9},{13,14},{14,13},{17,18},{18,... | collective-permute-start | bytes 786440 | tf_op jit(solution)/shard_map/ppermute | solution.py:519
  92.2 10.9 %collective-permute-start.25 = (f16[512,256]{1,0:T(8,128)(2,1)S(1)}, f16[512,256]{1,0:T(8,128)(2,1)S(1)}, u32[]{:S(2)}, u32[]{:S(2)}) collective-permute-start(f16[512,256]{1,0:T(8,128)(2,1)S(1)} %add_convert_fusion.1), channel_id=1, source_target_pairs={{1,0},{2,3},{5,4},{6,7},{9,8},{10,11},{13,12},{14,15},{17,16},{18,... | collective-permute-start | bytes 786440 | tf_op jit(solution)/shard_map/ppermute | solution.py:523
  99.6 10.6 %collective-permute-start.30 = (f16[512,256]{1,0:T(8,128)(2,1)S(1)}, f16[512,256]{1,0:T(8,128)(2,1)S(1)}, u32[]{:S(2)}, u32[]{:S(2)}) collective-permute-start(f16[512,256]{1,0:T(8,128)(2,1)S(1)} %add_convert_fusion), channel_id=1, source_target_pairs={{1,0},{2,3},{5,4},{6,7},{9,8},{10,11},{13,12},{14,15},{17,16},{18,... | collective-permute-start | bytes 786440 | tf_op jit(solution)/shard_map/ppermute | solution.py:523
  101.0 6.0 %collective-permute-start.31 = (f32[128,256]{1,0:T(8,128)S(1)}, f32[128,256]{1,0:T(8,128)S(1)}, u32[]{:S(2)}, u32[]{:S(2)}) collective-permute-start(f32[128,256]{1,0:T(8,128)S(1)} %select_add_fusion.1), channel_id=1, source_target_pairs={{0,8},{8,0},{4,12},{12,4},{1,9},{9,1},{5,13},{13,5},{2,10},{10,2},... | collective-permute-start | bytes 393224 | tf_op jit(solution)/shard_map/ppermute | solution.py:325
  112.5 3.4 %collective-permute-start.34 = (f32[128,256]{1,0:T(8,128)S(1)}, f32[128,256]{1,0:T(8,128)S(1)}, u32[]{:S(2)}, u32[]{:S(2)}) collective-permute-start(f32[128,256]{1,0:T(8,128)S(1)} %add.128), channel_id=1, source_target_pairs={{0,4},{4,0},{8,12},{12,8},{1,5},{5,1},{9,13},{13,9},{2,6},{6,2},{1... | collective-permute-start | bytes 393224 | tf_op jit(solution)/shard_map/ppermute | solution.py:321
  114.0 15.1 %collective-permute-start.33 = (f32[128,512]{1,0:T(8,128)S(1)}, f32[128,512]{1,0:T(8,128)S(1)}, u32[]{:S(2)}, u32[]{:S(2)}) collective-permute-start(f32[128,512]{1,0:T(8,128)S(1)} %select_add_fusion), channel_id=1, source_target_pairs={{0,8},{8,0},{4,12},{12,4},{1,9},{9,1},{5,13},{13,5},{2,10},{10,2},... | collective-permute-start | bytes 786440 | tf_op jit(solution)/shard_map/ppermute | solution.py:325
  (8 other events, 17.9 us)
where the time goes:
time: 147 us; the launch traced here: 146 us
  starting transfers between devices  44.1 us (30%)
  Pallas kernels  39.9 us (27%)
  waiting for transfers between devices  37.9 us (26%)
  matrix products  15.1 us (10%)
  other arithmetic  8.31 us (6%)
    pallas_call x2, Pallas kernels, solve_call(): pl.pallas_call(kernel, out_shape=shapes[0] if single else shapes, in_spec...  28.8 us
    ppermute x11, waiting for transfers between devices, over_y(): return lax.ppermute(values, 'blk', SWAP_Y)  17.1 us
    ppermute x11, starting transfers between devices, over_y(): return lax.ppermute(values, 'blk', SWAP_Y)  16.3 us
    pallas_call x3, Pallas kernels, tile_call(): pl.pallas_call(functools.partial(tile_kernel, exponent_scale, len(halves)...  10.5 us
    ppermute x4, starting transfers between devices, panel(): outers[i] = lax.ppermute(panels[i], 'dp', TO_INNER)  10 us
    ppermute x4, waiting for transfers between devices, total(): givens[i] = lax.ppermute(totals[i], 'dp', TO_OUTER)  7.26 us
    dot_general x8, matrix products, part_of(): lax.dot_general(tile, centred, (((0,), (0,)), ((), ())), preferred_elemen...  6.18 us
    ppermute x4, starting transfers between devices, total(): givens[i] = lax.ppermute(totals[i], 'dp', TO_OUTER)  5.39 us
  transfers between devices with their start and end apart: 36, of which 18 were waited for; matrix products, arithmetic and copies ran while one was open for 15% of the time, Pallas kernels for 17%

commit v1 on v0

--- a/solution.py
+++ b/solution.py
@@ -79,7 +79,7 @@
 
 def lower_inverse(square_ref, inverse_ref):
     groups = square_ref.shape[0] // PANEL
-    spans = 4
+    spans = 8
 
     for low in range(0, groups, groups // spans):
 
@@ -369,6 +369,26 @@
     )(stats, near_rows, first_rows, last_rows)
 
 
+def gram_kernel(upper_ref, lower_ref, out_ref):
+    upper, lower = upper_ref[...], lower_ref[...]
+    out_ref[...] = product_of(upper, upper) + product_of(lower, lower)
+
+
+def gram_call(upper, lower):
+    rows, order = upper.shape
+    vmem = pl.BlockSpec(memory_space=pltpu.VMEM)
+    return pl.pallas_call(
+        gram_kernel,
+        out_shape=jax.ShapeDtypeStruct((order, order), jnp.float32),
+        in_specs=[vmem, vmem],
+        out_specs=vmem,
+        compiler_params=pltpu.CompilerParams(vmem_limit_bytes=16 * 2**20),
+        cost_estimate=pl.CostEstimate(
+            flops=24 * rows * order * order, bytes_accessed=8 * rows * order, transcendentals=0
+        ),
+    )(upper, lower)
+
+
 def as_half(values):
     return lax.optimization_barrier(values.astype(jnp.float16))
 
@@ -545,7 +565,7 @@
     final(0)
     final(1)
     first = jnp.concatenate(finals[:2], 0)
-    kept, sent = split_step(ordered(product_of, first, first))
+    kept, sent = split_step(ordered(gram_call, *finals[:2]))
     arriving = over_cores(sent)
     total(3)
     kept = ordered(add_step, arriving, kept)

time: 147 us -> 145 us (0.986)
  matrix products: 15.1 us -> 13.3 us
    dot_general x2 -> x1, matrix products: 3.8 us -> 1.95 us  [product_of(): lax.dot_general(left, right, (((0,), (0,)), ((), ())), precision=HIGHEST)]
  transfers between devices with their start and end apart: 36 -> 36, of which waited for: 18 -> 18; matrix products, arithmetic and copies ran while one was open for 15% -> 14% of each run, Pallas kernels for 17% -> 17%
where the time goes in v1:
time: 145 us
  starting transfers between devices  44.2 us (30%)
  Pallas kernels  40.4 us (28%)
  waiting for transfers between devices  37.5 us (26%)
  matrix products  13.3 us (9%)
  other arithmetic  8.31 us (6%)
    pallas_call x2, Pallas kernels, solve_call(): pl.pallas_call(kernel, out_shape=shapes[0] if single else shapes, in_spec...  28 us
    ppermute x11, waiting for transfers between devices, over_y(): return lax.ppermute(values, 'blk', SWAP_Y)  16.6 us
    ppermute x11, starting transfers between devices, over_y(): return lax.ppermute(values, 'blk', SWAP_Y)  16.4 us
    pallas_call x3, Pallas kernels, tile_call(): pl.pallas_call(functools.partial(tile_kernel, exponent_scale, len(halves)...  10.5 us
    ppermute x4, starting transfers between devices, panel(): outers[i] = lax.ppermute(panels[i], 'dp', TO_INNER)  10 us
    ppermute x4, waiting for transfers between devices, total(): givens[i] = lax.ppermute(totals[i], 'dp', TO_OUTER)  7.53 us
    dot_general x8, matrix products, part_of(): lax.dot_general(tile, centred, (((0,), (0,)), ((), ())), preferred_elemen...  6.18 us
    ppermute x4, starting transfers between devices, total(): givens[i] = lax.ppermute(totals[i], 'dp', TO_OUTER)  5.39 us
  transfers between devices with their start and end apart: 36, of which 18 were waited for; matrix products, arithmetic and copies ran while one was open for 14% of the time, Pallas kernels for 17%

profile of v1, /device:TPU:0, one launch (start us, length us, event | category | flops | bytes accessed | tf_op | source)
XLA Modules:
  0.0 144.8 jit_solution(2616849554402691579)
XLA Ops:
  1.6 2.7 %collective-permute-start.1 = (bf16[512,384]{1,0:T(8,128)(2,1)S(1)}, bf16[512,384]{1,0:T(8,128)(2,1)S(1)}, u32[]{:S(2)}, u32[]{:S(2)}) collective-permute-start(bf16[512,384]{1,0:T(8,128)(2,1)S(1)} %slice_select_fusion.1), channel_id=1, source_target_pairs={{0,8},{8,0},{4,12},{12,4},{1,9},{9,1},{5,13},{13,5},{2,10},{10,2},... | collective-permute-start | bytes 1179656 | tf_op jit(solution)/shard_map/ppermute | solution.py:325
  4.5 2.2 %collective-permute-start.2 = (bf16[512,384]{1,0:T(8,128)(2,1)S(1)}, bf16[512,384]{1,0:T(8,128)(2,1)S(1)}, u32[]{:S(2)}, u32[]{:S(2)}) collective-permute-start(bf16[512,384]{1,0:T(8,128)(2,1)S(1)} %slice_select_fusion), channel_id=1, source_target_pairs={{0,8},{8,0},{4,12},{12,4},{1,9},{9,1},{5,13},{13,5},{2,10},{10,2},... | collective-permute-start | bytes 1179656 | tf_op jit(solution)/shard_map/ppermute | solution.py:325
  6.7 2.0 %fusion = f32[1920]{0:T(1024)S(1)} fusion(bf16[960,768]{1,0:T(8,128)(2,1)} %collective-permute-done, bf16[960,768]{1,0:T(8,128)(2,1)S(1)} %copy-done.2), kind=kLoop, calls=%fused_computation.2 | loop fusion | flops 8845440 | bytes 2956800 | tf_op jit(solution)/shard_map/reduce_sum | solution.py:27
  8.7 2.5 %fusion.1.data_ref = bf16[1920,768]{1,0:T(8,128)(2,1)S(1)} fusion(f32[1920]{0:T(1024)S(1)} %add_rsqrt_fusion, bf16[960,768]{1,0:T(8,128)(2,1)} %collective-permute-done, bf16[960,768]{1,0:T(8,128)(2,1)S(1)} %copy-done.2), kind=kLoop, calls=%fused_computation.3 | loop fusion | flops 8847360 | bytes 5905920 | tf_op jit(solution)/shard_map/convert_element_type | solution.py:27
  11.3 4.9 %shard_map.37 = (bf16[1920,1024]{1,0:T(8,128)(2,1)S(1)}, f32[2,1024]{1,0:T(2,128)S(1)}) custom-call(bf16[1920,768]{1,0:T(8,128)(2,1)S(1)} %fusion.1.data_ref, s32[1]{0:T(128)} %bitcast.odd_ref, bf16[1024,768]{1,0:T(8,128)(2,1)S(1)} %copy-done.1), custom_call_target="tpu_custom_call" | custom-call | flops 3019898880 | bytes 6881280 | tf_op jit(solution)/shard_map/pallas_call | solution.py:302
  16.1 1.6 %collective-permute-start.3 = (bf16[512,384]{1,0:T(8,128)(2,1)S(1)}, bf16[512,384]{1,0:T(8,128)(2,1)S(1)}, u32[]{:S(2)}, u32[]{:S(2)}) collective-permute-start(bf16[512,384]{1,0:T(8,128)(2,1)S(1)} %collective-permute-done.1.refs_0_), channel_id=1, source_target_pairs={{0,1},{1,0},{2,3},{3,2},{4,5},{5,4},{6,7},{7,6},{8,9},{9,8},{10,11... | collective-permute-start | bytes 1179656 | tf_op jit(solution)/shard_map/ppermute | solution.py:422
  20.8 1.6 %collective-permute-start.4 = (bf16[1024,256]{1,0:T(8,128)(2,1)S(1)}, bf16[1024,256]{1,0:T(8,128)(2,1)S(1)}, u32[]{:S(2)}, u32[]{:S(2)}) collective-permute-start(bf16[1024,256]{1,0:T(8,128)(2,1)S(1)} %get-tuple-element.64), channel_id=1, source_target_pairs={{0,8},{8,0},{4,12},{12,4},{1,9},{9,1},{5,13},{13,5},{2,10},{10,2},... | collective-permute-start | bytes 1572872 | tf_op jit(solution)/shard_map/ppermute | solution.py:325
  22.7 2.0 %collective-permute-start.6 = (bf16[512,384]{1,0:T(8,128)(2,1)S(1)}, bf16[512,384]{1,0:T(8,128)(2,1)S(1)}, u32[]{:S(2)}, u32[]{:S(2)}) collective-permute-start(bf16[512,384]{1,0:T(8,128)(2,1)S(1)} %collective-permute-done.2.refs_0_), channel_id=1, source_target_pairs={{0,1},{1,0},{2,3},{3,2},{4,5},{5,4},{6,7},{7,6},{8,9},{9,8},{10,11... | collective-permute-start | bytes 1179656 | tf_op jit(solution)/shard_map/ppermute | solution.py:422
  24.7 3.5 %collective-permute-done.3.refs_1_ = bf16[512,384]{1,0:T(8,128)(2,1)S(1)} collective-permute-done((bf16[512,384]{1,0:T(8,128)(2,1)S(1)}, bf16[512,384]{1,0:T(8,128)(2,1)S(1)}, u32[]{:S(2)}, u32[]{:S(2)}) %collective-permute-start.3) | collective-permute-done | bytes 393248 | tf_op jit(solution)/shard_map/ppermute | solution.py:422
  28.2 2.7 %shard_map.38 = (bf16[1920,512]{1,0:T(8,128)(2,1)S(1)}, f32[2,512]{1,0:T(2,128)S(1)}) custom-call(bf16[1920,768]{1,0:T(8,128)(2,1)S(1)} %fusion.1.data_ref, s32[1]{0:T(128)} %bitcast.odd_ref, bf16[512,384]{1,0:T(8,128)(2,1)S(1)} %collective-permute-done.1.refs_0_, bf16[512,384]{1,0:T(8,128)(2,1)S(1)} %collective-permute-done.3.refs_1_), custom_call_target="tpu_custom_call" | custom-call | flops 1509949440 | bytes 4915200 | tf_op jit(solution)/shard_map/pallas_call | solution.py:302
  30.9 3.0 %collective-permute-done.5.first_ref = bf16[1024,256]{1,0:T(8,128)(2,1)S(1)} collective-permute-done((bf16[1024,256]{1,0:T(8,128)(2,1)S(1)}, bf16[1024,256]{1,0:T(8,128)(2,1)S(1)}, u32[]{:S(2)}, u32[]{:S(2)}) %collective-permute-start.5) | collective-permute-done | bytes 524320 | tf_op jit(solution)/shard_map/ppermute | solution.py:325
  35.5 2.9 %shard_map.39 = (bf16[1920,512]{1,0:T(8,128)(2,1)S(1)}, f32[2,512]{1,0:T(2,128)S(1)}) custom-call(bf16[1920,768]{1,0:T(8,128)(2,1)S(1)} %fusion.1.data_ref, s32[1]{0:T(128)} %bitcast.odd_ref, bf16[512,384]{1,0:T(8,128)(2,1)S(1)} %collective-permute-done.2.refs_0_, bf16[512,384]{1,0:T(8,128)(2,1)S(1)} %collective-permute-done.6.refs_1_), custom_call_target="tpu_custom_call" | custom-call | flops 1509949440 | bytes 4915200 | tf_op jit(solution)/shard_map/pallas_call | solution.py:302
  38.4 1.7 %collective-permute-start.7 = (f32[2,2048]{1,0:T(2,128)S(1)}, f32[2,2048]{1,0:T(2,128)S(1)}, u32[]{:S(2)}, u32[]{:S(2)}) collective-permute-start(f32[2,2048]{1,0:T(2,128)S(1)} %constant_dynamic-update-slice_fusion), channel_id=1, source_target_pairs={{0,1},{1,0},{2,3},{3,2},{4,5},{5,4},{6,7},{7,6},{8,9},{9,8},{10,11... | collective-permute-start | bytes 49160 | tf_op jit(solution)/shard_map/ppermute | solution.py:463
  40.1 2.6 %collective-permute-start.8 = (f32[2,2048]{1,0:T(2,128)S(1)}, f32[2,2048]{1,0:T(2,128)S(1)}, u32[]{:S(2)}, u32[]{:S(2)}) collective-permute-start(f32[2,2048]{1,0:T(2,128)S(1)} %constant_dynamic-update-slice_fusion), channel_id=1, source_target_pairs={{0,2},{2,0},{1,3},{3,1},{4,6},{6,4},{5,7},{7,5},{8,10},{10,8},{9,1... | collective-permute-start | bytes 49160 | tf_op jit(solution)/shard_map/ppermute | solution.py:463
  44.8 3.4 %collective-permute-done.9 = f32[2,2048]{1,0:T(2,128)S(1)} collective-permute-done((f32[2,2048]{1,0:T(2,128)S(1)}, f32[2,2048]{1,0:T(2,128)S(1)}, u32[]{:S(2)}, u32[]{:S(2)}) %collective-permute-start.9) | collective-permute-done | bytes 16416 | tf_op jit(solution)/shard_map/ppermute | solution.py:463
  50.1 1.9 %collective-permute-done.10 = f32[2,2048]{1,0:T(2,128)S(1)} collective-permute-done((f32[2,2048]{1,0:T(2,128)S(1)}, f32[2,2048]{1,0:T(2,128)S(1)}, u32[]{:S(2)}, u32[]{:S(2)}) %collective-permute-start.10) | collective-permute-done | bytes 16416 | tf_op jit(solution)/shard_map/ppermute | solution.py:325
  59.1 5.8 %collective-permute-done.14 = f16[512,256]{1,0:T(8,128)(2,1)S(1)} collective-permute-done((f16[512,256]{1,0:T(8,128)(2,1)S(1)}, f16[512,256]{1,0:T(8,128)(2,1)S(1)}, u32[]{:S(2)}, u32[]{:S(2)}) %collective-permute-start.14) | collective-permute-done | bytes 262176 | tf_op jit(solution)/shard_map/ppermute | solution.py:325
  65.6 1.3 collective-permute-start.16
  68.9 1.5 %collective-permute-done.17 = f16[512,256]{1,0:T(8,128)(2,1)S(1)} collective-permute-done((f16[512,256]{1,0:T(8,128)(2,1)S(1)}, f16[512,256]{1,0:T(8,128)(2,1)S(1)}, u32[]{:S(2)}, u32[]{:S(2)}) %collective-permute-start.17) | collective-permute-done | bytes 262176 | tf_op jit(solution)/shard_map/ppermute | solution.py:325
  76.8 2.8 %collective-permute-start.18 = (f16[512,256]{1,0:T(8,128)(2,1)S(1)}, f16[512,256]{1,0:T(8,128)(2,1)S(1)}, u32[]{:S(2)}, u32[]{:S(2)}) collective-permute-start(f16[512,256]{1,0:T(8,128)(2,1)S(1)} %fusion.55), channel_id=1, source_target_pairs={{0,1},{3,2},{4,5},{7,6},{8,9},{11,10},{12,13},{15,14},{16,17},{19,... | collective-permute-start | bytes 786440 | tf_op jit(solution)/shard_map/ppermute | solution.py:535
  82.6 4.6 %collective-permute-start.23 = (f16[512,256]{1,0:T(8,128)(2,1)S(1)}, f16[512,256]{1,0:T(8,128)(2,1)S(1)}, u32[]{:S(2)}, u32[]{:S(2)}) collective-permute-start(f16[512,256]{1,0:T(8,128)(2,1)S(1)} %fusion.46), channel_id=1, source_target_pairs={{0,1},{3,2},{4,5},{7,6},{8,9},{11,10},{12,13},{15,14},{16,17},{19,... | collective-permute-start | bytes 786440 | tf_op jit(solution)/shard_map/ppermute | solution.py:535
  89.4 1.7 %collective-permute-done.23 = f16[512,256]{1,0:T(8,128)(2,1)S(1)} collective-permute-done((f16[512,256]{1,0:T(8,128)(2,1)S(1)}, f16[512,256]{1,0:T(8,128)(2,1)S(1)}, u32[]{:S(2)}, u32[]{:S(2)}) %collective-permute-start.23) | collective-permute-done | bytes 262176 | tf_op jit(solution)/shard_map/ppermute | solution.py:535
  93.4 3.8 %collective-permute-done.27 = f16[512,256]{1,0:T(8,128)(2,1)S(1)} collective-permute-done((f16[512,256]{1,0:T(8,128)(2,1)S(1)}, f16[512,256]{1,0:T(8,128)(2,1)S(1)}, u32[]{:S(2)}, u32[]{:S(2)}) %collective-permute-start.27) | collective-permute-done | bytes 262176 | tf_op jit(solution)/shard_map/ppermute | solution.py:543
  98.7 1.5 %collective-permute-start.30 = (f16[512,256]{1,0:T(8,128)(2,1)S(1)}, f16[512,256]{1,0:T(8,128)(2,1)S(1)}, u32[]{:S(2)}, u32[]{:S(2)}) collective-permute-start(f16[512,256]{1,0:T(8,128)(2,1)S(1)} %add_convert_fusion), channel_id=1, source_target_pairs={{1,0},{2,3},{5,4},{6,7},{9,8},{10,11},{13,12},{14,15},{17,16},{18,... | collective-permute-start | bytes 786440 | tf_op jit(solution)/shard_map/ppermute | solution.py:543
  100.3 1.8 %collective-permute-start.31 = (f32[128,256]{1,0:T(8,128)S(1)}, f32[128,256]{1,0:T(8,128)S(1)}, u32[]{:S(2)}, u32[]{:S(2)}) collective-permute-start(f32[128,256]{1,0:T(8,128)S(1)} %select_add_fusion.1), channel_id=1, source_target_pairs={{0,8},{8,0},{4,12},{12,4},{1,9},{9,1},{5,13},{13,5},{2,10},{10,2},... | collective-permute-start | bytes 393224 | tf_op jit(solution)/shard_map/ppermute | solution.py:325
  102.9 3.3 %collective-permute-done.31 = f32[128,256]{1,0:T(8,128)S(1)} collective-permute-done((f32[128,256]{1,0:T(8,128)S(1)}, f32[128,256]{1,0:T(8,128)S(1)}, u32[]{:S(2)}, u32[]{:S(2)}) %collective-permute-start.31) | collective-permute-done | bytes 131104 | tf_op jit(solution)/shard_map/ppermute | solution.py:325
  106.3 3.1 %collective-permute-done.30 = f16[512,256]{1,0:T(8,128)(2,1)S(1)} collective-permute-done((f16[512,256]{1,0:T(8,128)(2,1)S(1)}, f16[512,256]{1,0:T(8,128)(2,1)S(1)}, u32[]{:S(2)}, u32[]{:S(2)}) %collective-permute-start.30) | collective-permute-done | bytes 262176 | tf_op jit(solution)/shard_map/ppermute | solution.py:543
  109.5 2.0 %fusion.2 = f32[256,512]{1,0:T(8,128)S(1)} fusion(f32[512,256]{1,0:T(8,128)S(1)} %convert_multiply_fusion.2, f32[512,256]{1,0:T(8,128)S(1)} %convert_multiply_fusion.3, f32[512,256]{1,0:T(8,128)S(1)} %convert_multiply_fusion.4.lower_ref, f32[512,256]{1,0:T(8,128)S(1)} %convert_multiply_fusion.5.upper_ref), kind=kOutput, calls=%fused_computation.9 | convolution fusion | flops 1612447744 | bytes 2621440 | tf_op jit(solution)/shard_map/dot_general | solution.py:333
  113.1 1.8 %collective-permute-start.33 = (f32[128,512]{1,0:T(8,128)S(1)}, f32[128,512]{1,0:T(8,128)S(1)}, u32[]{:S(2)}, u32[]{:S(2)}) collective-permute-start(f32[128,512]{1,0:T(8,128)S(1)} %select_add_fusion), channel_id=1, source_target_pairs={{0,8},{8,0},{4,12},{12,4},{1,9},{9,1},{5,13},{13,5},{2,10},{10,2},... | collective-permute-start | bytes 786440 | tf_op jit(solution)/shard_map/ppermute | solution.py:325
  115.0 12.8 %shard_map.42 = (f32[1024,256]{1,0:T(8,128)S(1)}, f32[256,256]{1,0:T(8,128)S(1)}) custom-call(f32[256,256]{1,0:T(8,128)S(1)} %pad_maximum_fusion.5.gram_ref, f32[1024,256]{1,0:T(8,128)S(1)} %pad_maximum_fusion.2.rows_ref), custom_call_target="tpu_custom_call" | custom-call | flops 13421772800 | bytes 1310720 | tf_op jit(solution)/shard_map/pallas_call | solution.py:184
  128.0 1.4 collective-permute-done.35
  129.6 15.2 %shard_map.43 = f32[1024,512]{1,0:T(8,128)} custom-call(f32[256,512]{1,0:T(8,128)S(1)} %pad_maximum_fusion.3.gram_ref, f32[1024,256]{1,0:T(8,128)S(1)} %pad_maximum_fusion.1.rows_ref, f32[1024,256]{1,0:T(8,128)S(1)} %get-tuple-element.102.done_ref, f32[256,256]{1,0:T(8,128)S(1)} %get-tuple-element.104.solve_ref), custom_call_target="tpu_custom_call" | custom-call | flops 10737418240 | bytes 1048576 | tf_op jit(solution)/shard_map/pallas_call | solution.py:184
  (116 shorter events, 38.6 us)
Async XLA Ops:
  0.0 4.4 %collective-permute-start = (bf16[960,768]{1,0:T(8,128)(2,1)}, bf16[960,768]{1,0:T(8,128)(2,1)}, u32[]{:S(2)}, u32[]{:S(2)}) collective-permute-start(bf16[960,768]{1,0:T(8,128)(2,1)} %param.3), channel_id=1, source_target_pairs={{0,4},{4,0},{8,12},{12,8},{1,5},{5,1},{9,13},{13,9},{2,6},{6,2},{1... | collective-permute-start | bytes 4423688 | tf_op jit(solution)/shard_map/ppermute | solution.py:321
  1.6 14.5 %collective-permute-start.1 = (bf16[512,384]{1,0:T(8,128)(2,1)S(1)}, bf16[512,384]{1,0:T(8,128)(2,1)S(1)}, u32[]{:S(2)}, u32[]{:S(2)}) collective-permute-start(bf16[512,384]{1,0:T(8,128)(2,1)S(1)} %slice_select_fusion.1), channel_id=1, source_target_pairs={{0,8},{8,0},{4,12},{12,4},{1,9},{9,1},{5,13},{13,5},{2,10},{10,2},... | collective-permute-start | bytes 1179656 | tf_op jit(solution)/shard_map/ppermute | solution.py:325
  4.5 18.2 %collective-permute-start.2 = (bf16[512,384]{1,0:T(8,128)(2,1)S(1)}, bf16[512,384]{1,0:T(8,128)(2,1)S(1)}, u32[]{:S(2)}, u32[]{:S(2)}) collective-permute-start(bf16[512,384]{1,0:T(8,128)(2,1)S(1)} %slice_select_fusion), channel_id=1, source_target_pairs={{0,8},{8,0},{4,12},{12,4},{1,9},{9,1},{5,13},{13,5},{2,10},{10,2},... | collective-permute-start | bytes 1179656 | tf_op jit(solution)/shard_map/ppermute | solution.py:325
  16.1 12.1 %collective-permute-start.3 = (bf16[512,384]{1,0:T(8,128)(2,1)S(1)}, bf16[512,384]{1,0:T(8,128)(2,1)S(1)}, u32[]{:S(2)}, u32[]{:S(2)}) collective-permute-start(bf16[512,384]{1,0:T(8,128)(2,1)S(1)} %collective-permute-done.1.refs_0_), channel_id=1, source_target_pairs={{0,1},{1,0},{2,3},{3,2},{4,5},{5,4},{6,7},{7,6},{8,9},{9,8},{10,11... | collective-permute-start | bytes 1179656 | tf_op jit(solution)/shard_map/ppermute | solution.py:422
  19.0 14.9 %collective-permute-start.5 = (bf16[1024,256]{1,0:T(8,128)(2,1)S(1)}, bf16[1024,256]{1,0:T(8,128)(2,1)S(1)}, u32[]{:S(2)}, u32[]{:S(2)}) collective-permute-start(bf16[1024,256]{1,0:T(8,128)(2,1)S(1)} %get-tuple-element.67), channel_id=1, source_target_pairs={{0,8},{8,0},{4,12},{12,4},{1,9},{9,1},{5,13},{13,5},{2,10},{10,2},... | collective-permute-start | bytes 1572872 | tf_op jit(solution)/shard_map/ppermute | solution.py:325
  20.8 27.4 %collective-permute-start.4 = (bf16[1024,256]{1,0:T(8,128)(2,1)S(1)}, bf16[1024,256]{1,0:T(8,128)(2,1)S(1)}, u32[]{:S(2)}, u32[]{:S(2)}) collective-permute-start(bf16[1024,256]{1,0:T(8,128)(2,1)S(1)} %get-tuple-element.64), channel_id=1, source_target_pairs={{0,8},{8,0},{4,12},{12,4},{1,9},{9,1},{5,13},{13,5},{2,10},{10,2},... | collective-permute-start | bytes 1572872 | tf_op jit(solution)/shard_map/ppermute | solution.py:325
  22.7 12.8 %collective-permute-start.6 = (bf16[512,384]{1,0:T(8,128)(2,1)S(1)}, bf16[512,384]{1,0:T(8,128)(2,1)S(1)}, u32[]{:S(2)}, u32[]{:S(2)}) collective-permute-start(bf16[512,384]{1,0:T(8,128)(2,1)S(1)} %collective-permute-done.2.refs_0_), channel_id=1, source_target_pairs={{0,1},{1,0},{2,3},{3,2},{4,5},{5,4},{6,7},{7,6},{8,9},{9,8},{10,11... | collective-permute-start | bytes 1179656 | tf_op jit(solution)/shard_map/ppermute | solution.py:422
  38.4 5.2 %collective-permute-start.7 = (f32[2,2048]{1,0:T(2,128)S(1)}, f32[2,2048]{1,0:T(2,128)S(1)}, u32[]{:S(2)}, u32[]{:S(2)}) collective-permute-start(f32[2,2048]{1,0:T(2,128)S(1)} %constant_dynamic-update-slice_fusion), channel_id=1, source_target_pairs={{0,1},{1,0},{2,3},{3,2},{4,5},{5,4},{6,7},{7,6},{8,9},{9,8},{10,11... | collective-permute-start | bytes 49160 | tf_op jit(solution)/shard_map/ppermute | solution.py:463
  40.1 4.7 %collective-permute-start.8 = (f32[2,2048]{1,0:T(2,128)S(1)}, f32[2,2048]{1,0:T(2,128)S(1)}, u32[]{:S(2)}, u32[]{:S(2)}) collective-permute-start(f32[2,2048]{1,0:T(2,128)S(1)} %constant_dynamic-update-slice_fusion), channel_id=1, source_target_pairs={{0,2},{2,0},{1,3},{3,1},{4,6},{6,4},{5,7},{7,5},{8,10},{10,8},{9,1... | collective-permute-start | bytes 49160 | tf_op jit(solution)/shard_map/ppermute | solution.py:463
  42.6 5.5 %collective-permute-start.9 = (f32[2,2048]{1,0:T(2,128)S(1)}, f32[2,2048]{1,0:T(2,128)S(1)}, u32[]{:S(2)}, u32[]{:S(2)}) collective-permute-start(f32[2,2048]{1,0:T(2,128)S(1)} %constant_dynamic-update-slice_fusion), channel_id=1, source_target_pairs={{0,3},{3,0},{1,2},{2,1},{4,7},{7,4},{5,6},{6,5},{8,11},{11,8},{9,1... | collective-permute-start | bytes 49160 | tf_op jit(solution)/shard_map/ppermute | solution.py:463
  43.5 10.8 %collective-permute-start.13 = (f32[1920,256]{1,0:T(8,128)S(1)}, f32[1920,256]{1,0:T(8,128)S(1)}, u32[]{:S(2)}, u32[]{:S(2)}) collective-permute-start(f32[1920,256]{1,0:T(8,128)S(1)} %convolution_add_fusion), channel_id=1, source_target_pairs={{0,4},{4,0},{8,12},{12,8},{1,5},{5,1},{9,13},{13,9},{2,6},{6,2},{1... | collective-permute-start | bytes 5898248 | tf_op jit(solution)/shard_map/ppermute | solution.py:321
  48.2 3.8 %collective-permute-start.10 = (f32[2,2048]{1,0:T(2,128)S(1)}, f32[2,2048]{1,0:T(2,128)S(1)}, u32[]{:S(2)}, u32[]{:S(2)}) collective-permute-start(f32[2,2048]{1,0:T(2,128)S(1)} %pad_maximum_fusion.6), channel_id=1, source_target_pairs={{0,8},{8,0},{4,12},{12,4},{1,9},{9,1},{5,13},{13,5},{2,10},{10,2},... | collective-permute-start | bytes 49160 | tf_op jit(solution)/shard_map/ppermute | solution.py:325
  54.0 4.6 %collective-permute-start.12 = (f32[1920,256]{1,0:T(8,128)S(1)}, f32[1920,256]{1,0:T(8,128)S(1)}, u32[]{:S(2)}, u32[]{:S(2)}) collective-permute-start(f32[1920,256]{1,0:T(8,128)S(1)} %convolution_add_fusion.2), channel_id=1, source_target_pairs={{0,4},{4,0},{8,12},{12,8},{1,5},{5,1},{9,13},{13,9},{2,6},{6,2},{1... | collective-permute-start | bytes 5898248 | tf_op jit(solution)/shard_map/ppermute | solution.py:321
  55.6 9.2 %collective-permute-start.14 = (f16[512,256]{1,0:T(8,128)(2,1)S(1)}, f16[512,256]{1,0:T(8,128)(2,1)S(1)}, u32[]{:S(2)}, u32[]{:S(2)}) collective-permute-start(f16[512,256]{1,0:T(8,128)(2,1)S(1)} %fusion.58), channel_id=1, source_target_pairs={{0,8},{8,0},{4,12},{12,4},{1,9},{9,1},{5,13},{13,5},{2,10},{10,2},... | collective-permute-start | bytes 786440 | tf_op jit(solution)/shard_map/ppermute | solution.py:325
  57.6 12.8 %collective-permute-start.17 = (f16[512,256]{1,0:T(8,128)(2,1)S(1)}, f16[512,256]{1,0:T(8,128)(2,1)S(1)}, u32[]{:S(2)}, u32[]{:S(2)}) collective-permute-start(f16[512,256]{1,0:T(8,128)(2,1)S(1)} %fusion.59), channel_id=1, source_target_pairs={{0,8},{8,0},{4,12},{12,4},{1,9},{9,1},{5,13},{13,5},{2,10},{10,2},... | collective-permute-start | bytes 786440 | tf_op jit(solution)/shard_map/ppermute | solution.py:325
  65.6 8.8 %collective-permute-start.16 = (f16[512,256]{1,0:T(8,128)(2,1)S(1)}, f16[512,256]{1,0:T(8,128)(2,1)S(1)}, u32[]{:S(2)}, u32[]{:S(2)}) collective-permute-start(f16[512,256]{1,0:T(8,128)(2,1)S(1)} %fusion.52), channel_id=1, source_target_pairs={{0,1},{3,2},{4,5},{7,6},{8,9},{11,10},{12,13},{15,14},{16,17},{19,... | collective-permute-start | bytes 786440 | tf_op jit(solution)/shard_map/ppermute | solution.py:535
  67.7 8.3 %collective-permute-start.15 = (f16[512,256]{1,0:T(8,128)(2,1)S(1)}, f16[512,256]{1,0:T(8,128)(2,1)S(1)}, u32[]{:S(2)}, u32[]{:S(2)}) collective-permute-start(f16[512,256]{1,0:T(8,128)(2,1)S(1)} %fusion.60), channel_id=1, source_target_pairs={{0,8},{8,0},{4,12},{12,4},{1,9},{9,1},{5,13},{13,5},{2,10},{10,2},... | collective-permute-start | bytes 786440 | tf_op jit(solution)/shard_map/ppermute | solution.py:325
  71.1 8.5 %collective-permute-start.21 = (f16[512,256]{1,0:T(8,128)(2,1)S(1)}, f16[512,256]{1,0:T(8,128)(2,1)S(1)}, u32[]{:S(2)}, u32[]{:S(2)}) collective-permute-start(f16[512,256]{1,0:T(8,128)(2,1)S(1)} %fusion.49), channel_id=1, source_target_pairs={{0,1},{3,2},{4,5},{7,6},{8,9},{11,10},{12,13},{15,14},{16,17},{19,... | collective-permute-start | bytes 786440 | tf_op jit(solution)/shard_map/ppermute | solution.py:535
  73.2 8.6 %collective-permute-start.19 = (f16[512,256]{1,0:T(8,128)(2,1)S(1)}, f16[512,256]{1,0:T(8,128)(2,1)S(1)}, u32[]{:S(2)}, u32[]{:S(2)}) collective-permute-start(f16[512,256]{1,0:T(8,128)(2,1)S(1)} %fusion.61), channel_id=1, source_target_pairs={{0,8},{8,0},{4,12},{12,4},{1,9},{9,1},{5,13},{13,5},{2,10},{10,2},... | collective-permute-start | bytes 786440 | tf_op jit(solution)/shard_map/ppermute | solution.py:325
  74.5 5.9 %collective-permute-start.20 = (f16[512,256]{1,0:T(8,128)(2,1)S(1)}, f16[512,256]{1,0:T(8,128)(2,1)S(1)}, u32[]{:S(2)}, u32[]{:S(2)}) collective-permute-start(f16[512,256]{1,0:T(8,128)(2,1)S(1)} %add_convert_fusion.7), channel_id=1, source_target_pairs={{1,2},{2,1},{5,6},{6,5},{9,10},{10,9},{13,14},{14,13},{17,18},{18,... | collective-permute-start | bytes 786440 | tf_op jit(solution)/shard_map/ppermute | solution.py:539
  76.8 10.4 %collective-permute-start.18 = (f16[512,256]{1,0:T(8,128)(2,1)S(1)}, f16[512,256]{1,0:T(8,128)(2,1)S(1)}, u32[]{:S(2)}, u32[]{:S(2)}) collective-permute-start(f16[512,256]{1,0:T(8,128)(2,1)S(1)} %fusion.55), channel_id=1, source_target_pairs={{0,1},{3,2},{4,5},{7,6},{8,9},{11,10},{12,13},{15,14},{16,17},{19,... | collective-permute-start | bytes 786440 | tf_op jit(solution)/shard_map/ppermute | solution.py:535
  79.7 8.3 %collective-permute-start.24 = (f16[512,256]{1,0:T(8,128)(2,1)S(1)}, f16[512,256]{1,0:T(8,128)(2,1)S(1)}, u32[]{:S(2)}, u32[]{:S(2)}) collective-permute-start(f16[512,256]{1,0:T(8,128)(2,1)S(1)} %add_convert_fusion.6), channel_id=1, source_target_pairs={{1,2},{2,1},{5,6},{6,5},{9,10},{10,9},{13,14},{14,13},{17,18},{18,... | collective-permute-start | bytes 786440 | tf_op jit(solution)/shard_map/ppermute | solution.py:539
  80.5 12.7 %collective-permute-start.26 = (f16[512,256]{1,0:T(8,128)(2,1)S(1)}, f16[512,256]{1,0:T(8,128)(2,1)S(1)}, u32[]{:S(2)}, u32[]{:S(2)}) collective-permute-start(f16[512,256]{1,0:T(8,128)(2,1)S(1)} %add_convert_fusion.5), channel_id=1, source_target_pairs={{1,0},{2,3},{5,4},{6,7},{9,8},{10,11},{13,12},{14,15},{17,16},{18,... | collective-permute-start | bytes 786440 | tf_op jit(solution)/shard_map/ppermute | solution.py:543
  82.6 8.4 %collective-permute-start.23 = (f16[512,256]{1,0:T(8,128)(2,1)S(1)}, f16[512,256]{1,0:T(8,128)(2,1)S(1)}, u32[]{:S(2)}, u32[]{:S(2)}) collective-permute-start(f16[512,256]{1,0:T(8,128)(2,1)S(1)} %fusion.46), channel_id=1, source_target_pairs={{0,1},{3,2},{4,5},{7,6},{8,9},{11,10},{12,13},{15,14},{16,17},{19,... | collective-permute-start | bytes 786440 | tf_op jit(solution)/shard_map/ppermute | solution.py:535
  87.3 4.5 %collective-permute-start.22 = (f16[512,256]{1,0:T(8,128)(2,1)S(1)}, f16[512,256]{1,0:T(8,128)(2,1)S(1)}, u32[]{:S(2)}, u32[]{:S(2)}) collective-permute-start(f16[512,256]{1,0:T(8,128)(2,1)S(1)} %add_convert_fusion.4), channel_id=1, source_target_pairs={{1,2},{2,1},{5,6},{6,5},{9,10},{10,9},{13,14},{14,13},{17,18},{18,... | collective-permute-start | bytes 786440 | tf_op jit(solution)/shard_map/ppermute | solution.py:539
  88.1 9.1 %collective-permute-start.27 = (f16[512,256]{1,0:T(8,128)(2,1)S(1)}, f16[512,256]{1,0:T(8,128)(2,1)S(1)}, u32[]{:S(2)}, u32[]{:S(2)}) collective-permute-start(f16[512,256]{1,0:T(8,128)(2,1)S(1)} %add_convert_fusion.3), channel_id=1, source_target_pairs={{1,0},{2,3},{5,4},{6,7},{9,8},{10,11},{13,12},{14,15},{17,16},{18,... | collective-permute-start | bytes 786440 | tf_op jit(solution)/shard_map/ppermute | solution.py:543
  91.1 7.5 %collective-permute-start.29 = (f16[512,256]{1,0:T(8,128)(2,1)S(1)}, f16[512,256]{1,0:T(8,128)(2,1)S(1)}, u32[]{:S(2)}, u32[]{:S(2)}) collective-permute-start(f16[512,256]{1,0:T(8,128)(2,1)S(1)} %add_convert_fusion.2), channel_id=1, source_target_pairs={{1,2},{2,1},{5,6},{6,5},{9,10},{10,9},{13,14},{14,13},{17,18},{18,... | collective-permute-start | bytes 786440 | tf_op jit(solution)/shard_map/ppermute | solution.py:539
  91.9 10.9 %collective-permute-start.25 = (f16[512,256]{1,0:T(8,128)(2,1)S(1)}, f16[512,256]{1,0:T(8,128)(2,1)S(1)}, u32[]{:S(2)}, u32[]{:S(2)}) collective-permute-start(f16[512,256]{1,0:T(8,128)(2,1)S(1)} %add_convert_fusion.1), channel_id=1, source_target_pairs={{1,0},{2,3},{5,4},{6,7},{9,8},{10,11},{13,12},{14,15},{17,16},{18,... | collective-permute-start | bytes 786440 | tf_op jit(solution)/shard_map/ppermute | solution.py:543
  98.7 10.6 %collective-permute-start.30 = (f16[512,256]{1,0:T(8,128)(2,1)S(1)}, f16[512,256]{1,0:T(8,128)(2,1)S(1)}, u32[]{:S(2)}, u32[]{:S(2)}) collective-permute-start(f16[512,256]{1,0:T(8,128)(2,1)S(1)} %add_convert_fusion), channel_id=1, source_target_pairs={{1,0},{2,3},{5,4},{6,7},{9,8},{10,11},{13,12},{14,15},{17,16},{18,... | collective-permute-start | bytes 786440 | tf_op jit(solution)/shard_map/ppermute | solution.py:543
  100.3 6.0 %collective-permute-start.31 = (f32[128,256]{1,0:T(8,128)S(1)}, f32[128,256]{1,0:T(8,128)S(1)}, u32[]{:S(2)}, u32[]{:S(2)}) collective-permute-start(f32[128,256]{1,0:T(8,128)S(1)} %select_add_fusion.1), channel_id=1, source_target_pairs={{0,8},{8,0},{4,12},{12,4},{1,9},{9,1},{5,13},{13,5},{2,10},{10,2},... | collective-permute-start | bytes 393224 | tf_op jit(solution)/shard_map/ppermute | solution.py:325
  111.6 3.3 %collective-permute-start.34 = (f32[128,256]{1,0:T(8,128)S(1)}, f32[128,256]{1,0:T(8,128)S(1)}, u32[]{:S(2)}, u32[]{:S(2)}) collective-permute-start(f32[128,256]{1,0:T(8,128)S(1)} %add.128), channel_id=1, source_target_pairs={{0,4},{4,0},{8,12},{12,8},{1,5},{5,1},{9,13},{13,9},{2,6},{6,2},{1... | collective-permute-start | bytes 393224 | tf_op jit(solution)/shard_map/ppermute | solution.py:321
  113.1 14.7 %collective-permute-start.33 = (f32[128,512]{1,0:T(8,128)S(1)}, f32[128,512]{1,0:T(8,128)S(1)}, u32[]{:S(2)}, u32[]{:S(2)}) collective-permute-start(f32[128,512]{1,0:T(8,128)S(1)} %select_add_fusion), channel_id=1, source_target_pairs={{0,8},{8,0},{4,12},{12,4},{1,9},{9,1},{5,13},{13,5},{2,10},{10,2},... | collective-permute-start | bytes 786440 | tf_op jit(solution)/shard_map/ppermute | solution.py:325
  (8 other events, 18.1 us)

commit v2 on v1

--- a/solution.py
+++ b/solution.py
@@ -292,7 +292,7 @@
         )
 
     none = jnp.zeros((1, unit_ref.shape[0]), jnp.float32)
-    stats_ref[...] = jnp.concatenate(lax.fori_loop(0, rows // step, add_rows, (none, none), unroll=2), 0)
+    stats_ref[...] = jnp.concatenate(lax.fori_loop(0, rows // step, add_rows, (none, none), unroll=4 if other_refs else 2), 0)
 
 
 def tile_call(unit_data, odd, halves, others, exponent_scale):

time: 145 us -> 159 us (1.097); the launches traced: 145 us -> 156 us
  starting transfers between devices: 44.2 us -> 55.2 us
    ppermute x4, starting transfers between devices: 10 us -> 21.2 us  [panel(): outers[i] = lax.ppermute(panels[i], 'dp', TO_INNER)]
  transfers between devices with their start and end apart: 36 -> 36, of which waited for: 18 -> 18; matrix products, arithmetic and copies ran while one was open for 14% -> 13% of each run, Pallas kernels for 17% -> 16%
where the time goes in v2:
time: 159 us; the launch traced here: 156 us
  starting transfers between devices  55.2 us (35%)
  Pallas kernels  39.8 us (25%)
  waiting for transfers between devices  38.5 us (24%)
  matrix products  13.3 us (8%)
  other arithmetic  8.31 us (5%)
    pallas_call x2, Pallas kernels, solve_call(): pl.pallas_call(kernel, out_shape=shapes[0] if single else shapes, in_spec...  28 us
    ppermute x4, starting transfers between devices, panel(): outers[i] = lax.ppermute(panels[i], 'dp', TO_INNER)  21.2 us
    ppermute x11, waiting for transfers between devices, over_y(): return lax.ppermute(values, 'blk', SWAP_Y)  17.3 us
    ppermute x11, starting transfers between devices, over_y(): return lax.ppermute(values, 'blk', SWAP_Y)  16.3 us
    pallas_call x3, Pallas kernels, tile_call(): pl.pallas_call(functools.partial(tile_kernel, exponent_scale, len(halves)...  9.89 us
    ppermute x4, waiting for transfers between devices, total(): givens[i] = lax.ppermute(totals[i], 'dp', TO_OUTER)  7.71 us
    dot_general x8, matrix products, part_of(): lax.dot_general(tile, centred, (((0,), (0,)), ((), ())), preferred_elemen...  6.18 us
    ppermute x4, starting transfers between devices, total(): givens[i] = lax.ppermute(totals[i], 'dp', TO_OUTER)  5.17 us
  transfers between devices with their start and end apart: 36, of which 18 were waited for; matrix products, arithmetic and copies ran while one was open for 13% of the time, Pallas kernels for 16%

profile of v2, /device:TPU:0, one launch (start us, length us, event | category | flops | bytes accessed | tf_op | source)
XLA Modules:
  0.0 156.3 jit_solution(17143661975861718331)
XLA Ops:
  1.6 2.7 %collective-permute-start.1 = (bf16[512,384]{1,0:T(8,128)(2,1)S(1)}, bf16[512,384]{1,0:T(8,128)(2,1)S(1)}, u32[]{:S(2)}, u32[]{:S(2)}) collective-permute-start(bf16[512,384]{1,0:T(8,128)(2,1)S(1)} %slice_select_fusion.1), channel_id=1, source_target_pairs={{0,8},{8,0},{4,12},{12,4},{1,9},{9,1},{5,13},{13,5},{2,10},{10,2},... | collective-permute-start | bytes 1179656 | tf_op jit(solution)/shard_map/ppermute | solution.py:325
  4.5 2.2 %collective-permute-start.2 = (bf16[512,384]{1,0:T(8,128)(2,1)S(1)}, bf16[512,384]{1,0:T(8,128)(2,1)S(1)}, u32[]{:S(2)}, u32[]{:S(2)}) collective-permute-start(bf16[512,384]{1,0:T(8,128)(2,1)S(1)} %slice_select_fusion), channel_id=1, source_target_pairs={{0,8},{8,0},{4,12},{12,4},{1,9},{9,1},{5,13},{13,5},{2,10},{10,2},... | collective-permute-start | bytes 1179656 | tf_op jit(solution)/shard_map/ppermute | solution.py:325
  6.7 2.0 %fusion = f32[1920]{0:T(1024)S(1)} fusion(bf16[960,768]{1,0:T(8,128)(2,1)} %collective-permute-done, bf16[960,768]{1,0:T(8,128)(2,1)S(1)} %copy-done.2), kind=kLoop, calls=%fused_computation.2 | loop fusion | flops 8845440 | bytes 2956800 | tf_op jit(solution)/shard_map/reduce_sum | solution.py:27
  8.7 2.5 %fusion.1.data_ref = bf16[1920,768]{1,0:T(8,128)(2,1)S(1)} fusion(f32[1920]{0:T(1024)S(1)} %add_rsqrt_fusion, bf16[960,768]{1,0:T(8,128)(2,1)} %collective-permute-done, bf16[960,768]{1,0:T(8,128)(2,1)S(1)} %copy-done.2), kind=kLoop, calls=%fused_computation.3 | loop fusion | flops 8847360 | bytes 5905920 | tf_op jit(solution)/shard_map/convert_element_type | solution.py:27
  11.3 4.9 %shard_map.37 = (bf16[1920,1024]{1,0:T(8,128)(2,1)S(1)}, f32[2,1024]{1,0:T(2,128)S(1)}) custom-call(bf16[1920,768]{1,0:T(8,128)(2,1)S(1)} %fusion.1.data_ref, s32[1]{0:T(128)} %bitcast.odd_ref, bf16[1024,768]{1,0:T(8,128)(2,1)S(1)} %copy-done.1), custom_call_target="tpu_custom_call" | custom-call | flops 3019898880 | bytes 6881280 | tf_op jit(solution)/shard_map/pallas_call | solution.py:302
  16.1 1.6 %collective-permute-start.3 = (bf16[512,384]{1,0:T(8,128)(2,1)S(1)}, bf16[512,384]{1,0:T(8,128)(2,1)S(1)}, u32[]{:S(2)}, u32[]{:S(2)}) collective-permute-start(bf16[512,384]{1,0:T(8,128)(2,1)S(1)} %collective-permute-done.1.refs_0_), channel_id=1, source_target_pairs={{0,1},{1,0},{2,3},{3,2},{4,5},{5,4},{6,7},{7,6},{8,9},{9,8},{10,11... | collective-permute-start | bytes 1179656 | tf_op jit(solution)/shard_map/ppermute | solution.py:422
  20.8 1.6 %collective-permute-start.4 = (bf16[1024,256]{1,0:T(8,128)(2,1)S(1)}, bf16[1024,256]{1,0:T(8,128)(2,1)S(1)}, u32[]{:S(2)}, u32[]{:S(2)}) collective-permute-start(bf16[1024,256]{1,0:T(8,128)(2,1)S(1)} %get-tuple-element.64), channel_id=1, source_target_pairs={{0,8},{8,0},{4,12},{12,4},{1,9},{9,1},{5,13},{13,5},{2,10},{10,2},... | collective-permute-start | bytes 1572872 | tf_op jit(solution)/shard_map/ppermute | solution.py:325
  22.7 2.0 %collective-permute-start.6 = (bf16[512,384]{1,0:T(8,128)(2,1)S(1)}, bf16[512,384]{1,0:T(8,128)(2,1)S(1)}, u32[]{:S(2)}, u32[]{:S(2)}) collective-permute-start(bf16[512,384]{1,0:T(8,128)(2,1)S(1)} %collective-permute-done.2.refs_0_), channel_id=1, source_target_pairs={{0,1},{1,0},{2,3},{3,2},{4,5},{5,4},{6,7},{7,6},{8,9},{9,8},{10,11... | collective-permute-start | bytes 1179656 | tf_op jit(solution)/shard_map/ppermute | solution.py:422
  24.7 3.5 %collective-permute-done.3.refs_1_ = bf16[512,384]{1,0:T(8,128)(2,1)S(1)} collective-permute-done((bf16[512,384]{1,0:T(8,128)(2,1)S(1)}, bf16[512,384]{1,0:T(8,128)(2,1)S(1)}, u32[]{:S(2)}, u32[]{:S(2)}) %collective-permute-start.3) | collective-permute-done | bytes 393248 | tf_op jit(solution)/shard_map/ppermute | solution.py:422
  28.2 2.4 %shard_map.38 = (bf16[1920,512]{1,0:T(8,128)(2,1)S(1)}, f32[2,512]{1,0:T(2,128)S(1)}) custom-call(bf16[1920,768]{1,0:T(8,128)(2,1)S(1)} %fusion.1.data_ref, s32[1]{0:T(128)} %bitcast.odd_ref, bf16[512,384]{1,0:T(8,128)(2,1)S(1)} %collective-permute-done.1.refs_0_, bf16[512,384]{1,0:T(8,128)(2,1)S(1)} %collective-permute-done.3.refs_1_), custom_call_target="tpu_custom_call" | custom-call | flops 1509949440 | bytes 4915200 | tf_op jit(solution)/shard_map/pallas_call | solution.py:302
  30.6 3.3 %collective-permute-done.5.first_ref = bf16[1024,256]{1,0:T(8,128)(2,1)S(1)} collective-permute-done((bf16[1024,256]{1,0:T(8,128)(2,1)S(1)}, bf16[1024,256]{1,0:T(8,128)(2,1)S(1)}, u32[]{:S(2)}, u32[]{:S(2)}) %collective-permute-start.5) | collective-permute-done | bytes 524320 | tf_op jit(solution)/shard_map/ppermute | solution.py:325
  35.5 2.6 %shard_map.39 = (bf16[1920,512]{1,0:T(8,128)(2,1)S(1)}, f32[2,512]{1,0:T(2,128)S(1)}) custom-call(bf16[1920,768]{1,0:T(8,128)(2,1)S(1)} %fusion.1.data_ref, s32[1]{0:T(128)} %bitcast.odd_ref, bf16[512,384]{1,0:T(8,128)(2,1)S(1)} %collective-permute-done.2.refs_0_, bf16[512,384]{1,0:T(8,128)(2,1)S(1)} %collective-permute-done.6.refs_1_), custom_call_target="tpu_custom_call" | custom-call | flops 1509949440 | bytes 4915200 | tf_op jit(solution)/shard_map/pallas_call | solution.py:302
  38.2 1.6 %collective-permute-start.7 = (f32[2,2048]{1,0:T(2,128)S(1)}, f32[2,2048]{1,0:T(2,128)S(1)}, u32[]{:S(2)}, u32[]{:S(2)}) collective-permute-start(f32[2,2048]{1,0:T(2,128)S(1)} %constant_dynamic-update-slice_fusion), channel_id=1, source_target_pairs={{0,1},{1,0},{2,3},{3,2},{4,5},{5,4},{6,7},{7,6},{8,9},{9,8},{10,11... | collective-permute-start | bytes 49160 | tf_op jit(solution)/shard_map/ppermute | solution.py:463
  39.8 2.6 %collective-permute-start.8 = (f32[2,2048]{1,0:T(2,128)S(1)}, f32[2,2048]{1,0:T(2,128)S(1)}, u32[]{:S(2)}, u32[]{:S(2)}) collective-permute-start(f32[2,2048]{1,0:T(2,128)S(1)} %constant_dynamic-update-slice_fusion), channel_id=1, source_target_pairs={{0,2},{2,0},{1,3},{3,1},{4,6},{6,4},{5,7},{7,5},{8,10},{10,8},{9,1... | collective-permute-start | bytes 49160 | tf_op jit(solution)/shard_map/ppermute | solution.py:463
  44.5 3.4 %collective-permute-done.9 = f32[2,2048]{1,0:T(2,128)S(1)} collective-permute-done((f32[2,2048]{1,0:T(2,128)S(1)}, f32[2,2048]{1,0:T(2,128)S(1)}, u32[]{:S(2)}, u32[]{:S(2)}) %collective-permute-start.9) | collective-permute-done | bytes 16416 | tf_op jit(solution)/shard_map/ppermute | solution.py:463
  49.9 1.9 %collective-permute-done.10 = f32[2,2048]{1,0:T(2,128)S(1)} collective-permute-done((f32[2,2048]{1,0:T(2,128)S(1)}, f32[2,2048]{1,0:T(2,128)S(1)}, u32[]{:S(2)}, u32[]{:S(2)}) %collective-permute-start.10) | collective-permute-done | bytes 16416 | tf_op jit(solution)/shard_map/ppermute | solution.py:325
  58.8 5.8 %collective-permute-done.14 = f16[512,256]{1,0:T(8,128)(2,1)S(1)} collective-permute-done((f16[512,256]{1,0:T(8,128)(2,1)S(1)}, f16[512,256]{1,0:T(8,128)(2,1)S(1)}, u32[]{:S(2)}, u32[]{:S(2)}) %collective-permute-start.14) | collective-permute-done | bytes 262176 | tf_op jit(solution)/shard_map/ppermute | solution.py:325
  65.4 1.3 collective-permute-start.16
  68.6 1.5 collective-permute-done.17
  70.9 1.3 collective-permute-start.21
  76.5 14.1 %collective-permute-start.18 = (f16[512,256]{1,0:T(8,128)(2,1)S(1)}, f16[512,256]{1,0:T(8,128)(2,1)S(1)}, u32[]{:S(2)}, u32[]{:S(2)}) collective-permute-start(f16[512,256]{1,0:T(8,128)(2,1)S(1)} %fusion.55), channel_id=1, source_target_pairs={{0,1},{3,2},{4,5},{7,6},{8,9},{11,10},{12,13},{15,14},{16,17},{19,... | collective-permute-start | bytes 786440 | tf_op jit(solution)/shard_map/ppermute | solution.py:535
  93.6 4.6 %collective-permute-start.23 = (f16[512,256]{1,0:T(8,128)(2,1)S(1)}, f16[512,256]{1,0:T(8,128)(2,1)S(1)}, u32[]{:S(2)}, u32[]{:S(2)}) collective-permute-start(f16[512,256]{1,0:T(8,128)(2,1)S(1)} %fusion.46), channel_id=1, source_target_pairs={{0,1},{3,2},{4,5},{7,6},{8,9},{11,10},{12,13},{15,14},{16,17},{19,... | collective-permute-start | bytes 786440 | tf_op jit(solution)/shard_map/ppermute | solution.py:535
  100.4 1.7 %collective-permute-done.23 = f16[512,256]{1,0:T(8,128)(2,1)S(1)} collective-permute-done((f16[512,256]{1,0:T(8,128)(2,1)S(1)}, f16[512,256]{1,0:T(8,128)(2,1)S(1)}, u32[]{:S(2)}, u32[]{:S(2)}) %collective-permute-start.23) | collective-permute-done | bytes 262176 | tf_op jit(solution)/shard_map/ppermute | solution.py:535
  104.4 4.1 %collective-permute-done.27 = f16[512,256]{1,0:T(8,128)(2,1)S(1)} collective-permute-done((f16[512,256]{1,0:T(8,128)(2,1)S(1)}, f16[512,256]{1,0:T(8,128)(2,1)S(1)}, u32[]{:S(2)}, u32[]{:S(2)}) %collective-permute-start.27) | collective-permute-done | bytes 262176 | tf_op jit(solution)/shard_map/ppermute | solution.py:543
  111.4 1.8 %collective-permute-start.31 = (f32[128,256]{1,0:T(8,128)S(1)}, f32[128,256]{1,0:T(8,128)S(1)}, u32[]{:S(2)}, u32[]{:S(2)}) collective-permute-start(f32[128,256]{1,0:T(8,128)S(1)} %select_add_fusion.1), channel_id=1, source_target_pairs={{0,8},{8,0},{4,12},{12,4},{1,9},{9,1},{5,13},{13,5},{2,10},{10,2},... | collective-permute-start | bytes 393224 | tf_op jit(solution)/shard_map/ppermute | solution.py:325
  113.7 3.7 %collective-permute-done.31 = f32[128,256]{1,0:T(8,128)S(1)} collective-permute-done((f32[128,256]{1,0:T(8,128)S(1)}, f32[128,256]{1,0:T(8,128)S(1)}, u32[]{:S(2)}, u32[]{:S(2)}) %collective-permute-start.31) | collective-permute-done | bytes 131104 | tf_op jit(solution)/shard_map/ppermute | solution.py:325
  117.4 3.3 %collective-permute-done.30 = f16[512,256]{1,0:T(8,128)(2,1)S(1)} collective-permute-done((f16[512,256]{1,0:T(8,128)(2,1)S(1)}, f16[512,256]{1,0:T(8,128)(2,1)S(1)}, u32[]{:S(2)}, u32[]{:S(2)}) %collective-permute-start.30) | collective-permute-done | bytes 262176 | tf_op jit(solution)/shard_map/ppermute | solution.py:543
  120.8 2.0 %fusion.2 = f32[256,512]{1,0:T(8,128)S(1)} fusion(f32[512,256]{1,0:T(8,128)S(1)} %convert_multiply_fusion.2, f32[512,256]{1,0:T(8,128)S(1)} %convert_multiply_fusion.3, f32[512,256]{1,0:T(8,128)S(1)} %convert_multiply_fusion.4.lower_ref, f32[512,256]{1,0:T(8,128)S(1)} %convert_multiply_fusion.5.upper_ref), kind=kOutput, calls=%fused_computation.9 | convolution fusion | flops 1612447744 | bytes 2621440 | tf_op jit(solution)/shard_map/dot_general | solution.py:333
  124.5 1.8 %collective-permute-start.33 = (f32[128,512]{1,0:T(8,128)S(1)}, f32[128,512]{1,0:T(8,128)S(1)}, u32[]{:S(2)}, u32[]{:S(2)}) collective-permute-start(f32[128,512]{1,0:T(8,128)S(1)} %select_add_fusion), channel_id=1, source_target_pairs={{0,8},{8,0},{4,12},{12,4},{1,9},{9,1},{5,13},{13,5},{2,10},{10,2},... | collective-permute-start | bytes 786440 | tf_op jit(solution)/shard_map/ppermute | solution.py:325
  126.3 12.8 %shard_map.42 = (f32[1024,256]{1,0:T(8,128)S(1)}, f32[256,256]{1,0:T(8,128)S(1)}) custom-call(f32[256,256]{1,0:T(8,128)S(1)} %pad_maximum_fusion.5.gram_ref, f32[1024,256]{1,0:T(8,128)S(1)} %pad_maximum_fusion.2.rows_ref), custom_call_target="tpu_custom_call" | custom-call | flops 13421772800 | bytes 1310720 | tf_op jit(solution)/shard_map/pallas_call | solution.py:184
  139.4 1.4 collective-permute-done.35
  140.9 15.2 %shard_map.43 = f32[1024,512]{1,0:T(8,128)} custom-call(f32[256,512]{1,0:T(8,128)S(1)} %pad_maximum_fusion.3.gram_ref, f32[1024,256]{1,0:T(8,128)S(1)} %pad_maximum_fusion.1.rows_ref, f32[1024,256]{1,0:T(8,128)S(1)} %get-tuple-element.102.done_ref, f32[256,256]{1,0:T(8,128)S(1)} %get-tuple-element.104.solve_ref), custom_call_target="tpu_custom_call" | custom-call | flops 10737418240 | bytes 1048576 | tf_op jit(solution)/shard_map/pallas_call | solution.py:184
  (116 shorter events, 38.2 us)
Async XLA Ops:
  0.0 4.4 %collective-permute-start = (bf16[960,768]{1,0:T(8,128)(2,1)}, bf16[960,768]{1,0:T(8,128)(2,1)}, u32[]{:S(2)}, u32[]{:S(2)}) collective-permute-start(bf16[960,768]{1,0:T(8,128)(2,1)} %param.3), channel_id=1, source_target_pairs={{0,4},{4,0},{8,12},{12,8},{1,5},{5,1},{9,13},{13,9},{2,6},{6,2},{1... | collective-permute-start | bytes 4423688 | tf_op jit(solution)/shard_map/ppermute | solution.py:321
  1.6 14.5 %collective-permute-start.1 = (bf16[512,384]{1,0:T(8,128)(2,1)S(1)}, bf16[512,384]{1,0:T(8,128)(2,1)S(1)}, u32[]{:S(2)}, u32[]{:S(2)}) collective-permute-start(bf16[512,384]{1,0:T(8,128)(2,1)S(1)} %slice_select_fusion.1), channel_id=1, source_target_pairs={{0,8},{8,0},{4,12},{12,4},{1,9},{9,1},{5,13},{13,5},{2,10},{10,2},... | collective-permute-start | bytes 1179656 | tf_op jit(solution)/shard_map/ppermute | solution.py:325
  4.5 18.2 %collective-permute-start.2 = (bf16[512,384]{1,0:T(8,128)(2,1)S(1)}, bf16[512,384]{1,0:T(8,128)(2,1)S(1)}, u32[]{:S(2)}, u32[]{:S(2)}) collective-permute-start(bf16[512,384]{1,0:T(8,128)(2,1)S(1)} %slice_select_fusion), channel_id=1, source_target_pairs={{0,8},{8,0},{4,12},{12,4},{1,9},{9,1},{5,13},{13,5},{2,10},{10,2},... | collective-permute-start | bytes 1179656 | tf_op jit(solution)/shard_map/ppermute | solution.py:325
  16.1 12.1 %collective-permute-start.3 = (bf16[512,384]{1,0:T(8,128)(2,1)S(1)}, bf16[512,384]{1,0:T(8,128)(2,1)S(1)}, u32[]{:S(2)}, u32[]{:S(2)}) collective-permute-start(bf16[512,384]{1,0:T(8,128)(2,1)S(1)} %collective-permute-done.1.refs_0_), channel_id=1, source_target_pairs={{0,1},{1,0},{2,3},{3,2},{4,5},{5,4},{6,7},{7,6},{8,9},{9,8},{10,11... | collective-permute-start | bytes 1179656 | tf_op jit(solution)/shard_map/ppermute | solution.py:422
  19.0 14.9 %collective-permute-start.5 = (bf16[1024,256]{1,0:T(8,128)(2,1)S(1)}, bf16[1024,256]{1,0:T(8,128)(2,1)S(1)}, u32[]{:S(2)}, u32[]{:S(2)}) collective-permute-start(bf16[1024,256]{1,0:T(8,128)(2,1)S(1)} %get-tuple-element.67), channel_id=1, source_target_pairs={{0,8},{8,0},{4,12},{12,4},{1,9},{9,1},{5,13},{13,5},{2,10},{10,2},... | collective-permute-start | bytes 1572872 | tf_op jit(solution)/shard_map/ppermute | solution.py:325
  20.8 27.2 %collective-permute-start.4 = (bf16[1024,256]{1,0:T(8,128)(2,1)S(1)}, bf16[1024,256]{1,0:T(8,128)(2,1)S(1)}, u32[]{:S(2)}, u32[]{:S(2)}) collective-permute-start(bf16[1024,256]{1,0:T(8,128)(2,1)S(1)} %get-tuple-element.64), channel_id=1, source_target_pairs={{0,8},{8,0},{4,12},{12,4},{1,9},{9,1},{5,13},{13,5},{2,10},{10,2},... | collective-permute-start | bytes 1572872 | tf_op jit(solution)/shard_map/ppermute | solution.py:325
  22.7 12.8 %collective-permute-start.6 = (bf16[512,384]{1,0:T(8,128)(2,1)S(1)}, bf16[512,384]{1,0:T(8,128)(2,1)S(1)}, u32[]{:S(2)}, u32[]{:S(2)}) collective-permute-start(bf16[512,384]{1,0:T(8,128)(2,1)S(1)} %collective-permute-done.2.refs_0_), channel_id=1, source_target_pairs={{0,1},{1,0},{2,3},{3,2},{4,5},{5,4},{6,7},{7,6},{8,9},{9,8},{10,11... | collective-permute-start | bytes 1179656 | tf_op jit(solution)/shard_map/ppermute | solution.py:422
  38.2 5.2 %collective-permute-start.7 = (f32[2,2048]{1,0:T(2,128)S(1)}, f32[2,2048]{1,0:T(2,128)S(1)}, u32[]{:S(2)}, u32[]{:S(2)}) collective-permute-start(f32[2,2048]{1,0:T(2,128)S(1)} %constant_dynamic-update-slice_fusion), channel_id=1, source_target_pairs={{0,1},{1,0},{2,3},{3,2},{4,5},{5,4},{6,7},{7,6},{8,9},{9,8},{10,11... | collective-permute-start | bytes 49160 | tf_op jit(solution)/shard_map/ppermute | solution.py:463
  39.8 4.7 %collective-permute-start.8 = (f32[2,2048]{1,0:T(2,128)S(1)}, f32[2,2048]{1,0:T(2,128)S(1)}, u32[]{:S(2)}, u32[]{:S(2)}) collective-permute-start(f32[2,2048]{1,0:T(2,128)S(1)} %constant_dynamic-update-slice_fusion), channel_id=1, source_target_pairs={{0,2},{2,0},{1,3},{3,1},{4,6},{6,4},{5,7},{7,5},{8,10},{10,8},{9,1... | collective-permute-start | bytes 49160 | tf_op jit(solution)/shard_map/ppermute | solution.py:463
  42.4 5.5 %collective-permute-start.9 = (f32[2,2048]{1,0:T(2,128)S(1)}, f32[2,2048]{1,0:T(2,128)S(1)}, u32[]{:S(2)}, u32[]{:S(2)}) collective-permute-start(f32[2,2048]{1,0:T(2,128)S(1)} %constant_dynamic-update-slice_fusion), channel_id=1, source_target_pairs={{0,3},{3,0},{1,2},{2,1},{4,7},{7,4},{5,6},{6,5},{8,11},{11,8},{9,1... | collective-permute-start | bytes 49160 | tf_op jit(solution)/shard_map/ppermute | solution.py:463
  43.3 10.8 %collective-permute-start.13 = (f32[1920,256]{1,0:T(8,128)S(1)}, f32[1920,256]{1,0:T(8,128)S(1)}, u32[]{:S(2)}, u32[]{:S(2)}) collective-permute-start(f32[1920,256]{1,0:T(8,128)S(1)} %convolution_add_fusion), channel_id=1, source_target_pairs={{0,4},{4,0},{8,12},{12,8},{1,5},{5,1},{9,13},{13,9},{2,6},{6,2},{1... | collective-permute-start | bytes 5898248 | tf_op jit(solution)/shard_map/ppermute | solution.py:321
  48.0 3.8 %collective-permute-start.10 = (f32[2,2048]{1,0:T(2,128)S(1)}, f32[2,2048]{1,0:T(2,128)S(1)}, u32[]{:S(2)}, u32[]{:S(2)}) collective-permute-start(f32[2,2048]{1,0:T(2,128)S(1)} %pad_maximum_fusion.6), channel_id=1, source_target_pairs={{0,8},{8,0},{4,12},{12,4},{1,9},{9,1},{5,13},{13,5},{2,10},{10,2},... | collective-permute-start | bytes 49160 | tf_op jit(solution)/shard_map/ppermute | solution.py:325
  53.8 4.6 %collective-permute-start.12 = (f32[1920,256]{1,0:T(8,128)S(1)}, f32[1920,256]{1,0:T(8,128)S(1)}, u32[]{:S(2)}, u32[]{:S(2)}) collective-permute-start(f32[1920,256]{1,0:T(8,128)S(1)} %convolution_add_fusion.2), channel_id=1, source_target_pairs={{0,4},{4,0},{8,12},{12,8},{1,5},{5,1},{9,13},{13,9},{2,6},{6,2},{1... | collective-permute-start | bytes 5898248 | tf_op jit(solution)/shard_map/ppermute | solution.py:321
  55.4 9.2 %collective-permute-start.14 = (f16[512,256]{1,0:T(8,128)(2,1)S(1)}, f16[512,256]{1,0:T(8,128)(2,1)S(1)}, u32[]{:S(2)}, u32[]{:S(2)}) collective-permute-start(f16[512,256]{1,0:T(8,128)(2,1)S(1)} %fusion.58), channel_id=1, source_target_pairs={{0,8},{8,0},{4,12},{12,4},{1,9},{9,1},{5,13},{13,5},{2,10},{10,2},... | collective-permute-start | bytes 786440 | tf_op jit(solution)/shard_map/ppermute | solution.py:325
  57.3 12.8 %collective-permute-start.17 = (f16[512,256]{1,0:T(8,128)(2,1)S(1)}, f16[512,256]{1,0:T(8,128)(2,1)S(1)}, u32[]{:S(2)}, u32[]{:S(2)}) collective-permute-start(f16[512,256]{1,0:T(8,128)(2,1)S(1)} %fusion.59), channel_id=1, source_target_pairs={{0,8},{8,0},{4,12},{12,4},{1,9},{9,1},{5,13},{13,5},{2,10},{10,2},... | collective-permute-start | bytes 786440 | tf_op jit(solution)/shard_map/ppermute | solution.py:325
  65.4 8.8 %collective-permute-start.16 = (f16[512,256]{1,0:T(8,128)(2,1)S(1)}, f16[512,256]{1,0:T(8,128)(2,1)S(1)}, u32[]{:S(2)}, u32[]{:S(2)}) collective-permute-start(f16[512,256]{1,0:T(8,128)(2,1)S(1)} %fusion.52), channel_id=1, source_target_pairs={{0,1},{3,2},{4,5},{7,6},{8,9},{11,10},{12,13},{15,14},{16,17},{19,... | collective-permute-start | bytes 786440 | tf_op jit(solution)/shard_map/ppermute | solution.py:535
  67.5 8.3 %collective-permute-start.15 = (f16[512,256]{1,0:T(8,128)(2,1)S(1)}, f16[512,256]{1,0:T(8,128)(2,1)S(1)}, u32[]{:S(2)}, u32[]{:S(2)}) collective-permute-start(f16[512,256]{1,0:T(8,128)(2,1)S(1)} %fusion.60), channel_id=1, source_target_pairs={{0,8},{8,0},{4,12},{12,4},{1,9},{9,1},{5,13},{13,5},{2,10},{10,2},... | collective-permute-start | bytes 786440 | tf_op jit(solution)/shard_map/ppermute | solution.py:325
  70.9 19.7 %collective-permute-start.21 = (f16[512,256]{1,0:T(8,128)(2,1)S(1)}, f16[512,256]{1,0:T(8,128)(2,1)S(1)}, u32[]{:S(2)}, u32[]{:S(2)}) collective-permute-start(f16[512,256]{1,0:T(8,128)(2,1)S(1)} %fusion.49), channel_id=1, source_target_pairs={{0,1},{3,2},{4,5},{7,6},{8,9},{11,10},{12,13},{15,14},{16,17},{19,... | collective-permute-start | bytes 786440 | tf_op jit(solution)/shard_map/ppermute | solution.py:535
  73.0 19.8 %collective-permute-start.19 = (f16[512,256]{1,0:T(8,128)(2,1)S(1)}, f16[512,256]{1,0:T(8,128)(2,1)S(1)}, u32[]{:S(2)}, u32[]{:S(2)}) collective-permute-start(f16[512,256]{1,0:T(8,128)(2,1)S(1)} %fusion.61), channel_id=1, source_target_pairs={{0,8},{8,0},{4,12},{12,4},{1,9},{9,1},{5,13},{13,5},{2,10},{10,2},... | collective-permute-start | bytes 786440 | tf_op jit(solution)/shard_map/ppermute | solution.py:325
  74.2 17.1 %collective-permute-start.20 = (f16[512,256]{1,0:T(8,128)(2,1)S(1)}, f16[512,256]{1,0:T(8,128)(2,1)S(1)}, u32[]{:S(2)}, u32[]{:S(2)}) collective-permute-start(f16[512,256]{1,0:T(8,128)(2,1)S(1)} %add_convert_fusion.7), channel_id=1, source_target_pairs={{1,2},{2,1},{5,6},{6,5},{9,10},{10,9},{13,14},{14,13},{17,18},{18,... | collective-permute-start | bytes 786440 | tf_op jit(solution)/shard_map/ppermute | solution.py:539
  76.5 21.6 %collective-permute-start.18 = (f16[512,256]{1,0:T(8,128)(2,1)S(1)}, f16[512,256]{1,0:T(8,128)(2,1)S(1)}, u32[]{:S(2)}, u32[]{:S(2)}) collective-permute-start(f16[512,256]{1,0:T(8,128)(2,1)S(1)} %fusion.55), channel_id=1, source_target_pairs={{0,1},{3,2},{4,5},{7,6},{8,9},{11,10},{12,13},{15,14},{16,17},{19,... | collective-permute-start | bytes 786440 | tf_op jit(solution)/shard_map/ppermute | solution.py:535
  90.7 8.3 %collective-permute-start.24 = (f16[512,256]{1,0:T(8,128)(2,1)S(1)}, f16[512,256]{1,0:T(8,128)(2,1)S(1)}, u32[]{:S(2)}, u32[]{:S(2)}) collective-permute-start(f16[512,256]{1,0:T(8,128)(2,1)S(1)} %add_convert_fusion.6), channel_id=1, source_target_pairs={{1,2},{2,1},{5,6},{6,5},{9,10},{10,9},{13,14},{14,13},{17,18},{18,... | collective-permute-start | bytes 786440 | tf_op jit(solution)/shard_map/ppermute | solution.py:539
  91.5 12.7 %collective-permute-start.26 = (f16[512,256]{1,0:T(8,128)(2,1)S(1)}, f16[512,256]{1,0:T(8,128)(2,1)S(1)}, u32[]{:S(2)}, u32[]{:S(2)}) collective-permute-start(f16[512,256]{1,0:T(8,128)(2,1)S(1)} %add_convert_fusion.5), channel_id=1, source_target_pairs={{1,0},{2,3},{5,4},{6,7},{9,8},{10,11},{13,12},{14,15},{17,16},{18,... | collective-permute-start | bytes 786440 | tf_op jit(solution)/shard_map/ppermute | solution.py:543
  93.6 8.4 %collective-permute-start.23 = (f16[512,256]{1,0:T(8,128)(2,1)S(1)}, f16[512,256]{1,0:T(8,128)(2,1)S(1)}, u32[]{:S(2)}, u32[]{:S(2)}) collective-permute-start(f16[512,256]{1,0:T(8,128)(2,1)S(1)} %fusion.46), channel_id=1, source_target_pairs={{0,1},{3,2},{4,5},{7,6},{8,9},{11,10},{12,13},{15,14},{16,17},{19,... | collective-permute-start | bytes 786440 | tf_op jit(solution)/shard_map/ppermute | solution.py:535
  98.3 4.5 %collective-permute-start.22 = (f16[512,256]{1,0:T(8,128)(2,1)S(1)}, f16[512,256]{1,0:T(8,128)(2,1)S(1)}, u32[]{:S(2)}, u32[]{:S(2)}) collective-permute-start(f16[512,256]{1,0:T(8,128)(2,1)S(1)} %add_convert_fusion.4), channel_id=1, source_target_pairs={{1,2},{2,1},{5,6},{6,5},{9,10},{10,9},{13,14},{14,13},{17,18},{18,... | collective-permute-start | bytes 786440 | tf_op jit(solution)/shard_map/ppermute | solution.py:539
  99.1 9.4 %collective-permute-start.27 = (f16[512,256]{1,0:T(8,128)(2,1)S(1)}, f16[512,256]{1,0:T(8,128)(2,1)S(1)}, u32[]{:S(2)}, u32[]{:S(2)}) collective-permute-start(f16[512,256]{1,0:T(8,128)(2,1)S(1)} %add_convert_fusion.3), channel_id=1, source_target_pairs={{1,0},{2,3},{5,4},{6,7},{9,8},{10,11},{13,12},{14,15},{17,16},{18,... | collective-permute-start | bytes 786440 | tf_op jit(solution)/shard_map/ppermute | solution.py:543
  102.1 7.9 %collective-permute-start.29 = (f16[512,256]{1,0:T(8,128)(2,1)S(1)}, f16[512,256]{1,0:T(8,128)(2,1)S(1)}, u32[]{:S(2)}, u32[]{:S(2)}) collective-permute-start(f16[512,256]{1,0:T(8,128)(2,1)S(1)} %add_convert_fusion.2), channel_id=1, source_target_pairs={{1,2},{2,1},{5,6},{6,5},{9,10},{10,9},{13,14},{14,13},{17,18},{18,... | collective-permute-start | bytes 786440 | tf_op jit(solution)/shard_map/ppermute | solution.py:539
  102.9 10.6 %collective-permute-start.25 = (f16[512,256]{1,0:T(8,128)(2,1)S(1)}, f16[512,256]{1,0:T(8,128)(2,1)S(1)}, u32[]{:S(2)}, u32[]{:S(2)}) collective-permute-start(f16[512,256]{1,0:T(8,128)(2,1)S(1)} %add_convert_fusion.1), channel_id=1, source_target_pairs={{1,0},{2,3},{5,4},{6,7},{9,8},{10,11},{13,12},{14,15},{17,16},{18,... | collective-permute-start | bytes 786440 | tf_op jit(solution)/shard_map/ppermute | solution.py:543
  110.1 10.6 %collective-permute-start.30 = (f16[512,256]{1,0:T(8,128)(2,1)S(1)}, f16[512,256]{1,0:T(8,128)(2,1)S(1)}, u32[]{:S(2)}, u32[]{:S(2)}) collective-permute-start(f16[512,256]{1,0:T(8,128)(2,1)S(1)} %add_convert_fusion), channel_id=1, source_target_pairs={{1,0},{2,3},{5,4},{6,7},{9,8},{10,11},{13,12},{14,15},{17,16},{18,... | collective-permute-start | bytes 786440 | tf_op jit(solution)/shard_map/ppermute | solution.py:543
  111.4 6.0 %collective-permute-start.31 = (f32[128,256]{1,0:T(8,128)S(1)}, f32[128,256]{1,0:T(8,128)S(1)}, u32[]{:S(2)}, u32[]{:S(2)}) collective-permute-start(f32[128,256]{1,0:T(8,128)S(1)} %select_add_fusion.1), channel_id=1, source_target_pairs={{0,8},{8,0},{4,12},{12,4},{1,9},{9,1},{5,13},{13,5},{2,10},{10,2},... | collective-permute-start | bytes 393224 | tf_op jit(solution)/shard_map/ppermute | solution.py:325
  123.0 3.3 %collective-permute-start.34 = (f32[128,256]{1,0:T(8,128)S(1)}, f32[128,256]{1,0:T(8,128)S(1)}, u32[]{:S(2)}, u32[]{:S(2)}) collective-permute-start(f32[128,256]{1,0:T(8,128)S(1)} %add.128), channel_id=1, source_target_pairs={{0,4},{4,0},{8,12},{12,8},{1,5},{5,1},{9,13},{13,9},{2,6},{6,2},{1... | collective-permute-start | bytes 393224 | tf_op jit(solution)/shard_map/ppermute | solution.py:321
  124.5 14.7 %collective-permute-start.33 = (f32[128,512]{1,0:T(8,128)S(1)}, f32[128,512]{1,0:T(8,128)S(1)}, u32[]{:S(2)}, u32[]{:S(2)}) collective-permute-start(f32[128,512]{1,0:T(8,128)S(1)} %select_add_fusion), channel_id=1, source_target_pairs={{0,8},{8,0},{4,12},{12,4},{1,9},{9,1},{5,13},{13,5},{2,10},{10,2},... | collective-permute-start | bytes 786440 | tf_op jit(solution)/shard_map/ppermute | solution.py:325
  (8 other events, 17.9 us)

commit v3 on v1

--- a/solution.py
+++ b/solution.py
@@ -284,7 +284,7 @@
             (((1,), (1,)), ((), ())),
             preferred_element_type=jnp.float32,
         )
-        tile = jnp.exp(exponent_scale * scores).astype(jnp.bfloat16)
+        tile = jnp.exp2(exponent_scale * math.log2(math.e) * scores).astype(jnp.bfloat16)
         tile_ref[here, :] = tile
         wide = tile.astype(jnp.float32)
         return stats[0] + jnp.sum(wide, axis=0, keepdims=True), stats[1] + jnp.sum(

time: 145 us -> 145 us (level)
  transfers between devices with their start and end apart: 36 -> 36, of which waited for: 18 -> 18; matrix products, arithmetic and copies ran while one was open for 14% -> 14% of each run, Pallas kernels for 17% -> 18%
where the time goes in v3:
time: 145 us
  starting transfers between devices  43.8 us (30%)
  Pallas kernels  40.5 us (28%)
  waiting for transfers between devices  37.7 us (26%)
  matrix products  13.3 us (9%)
  other arithmetic  8.31 us (6%)
    pallas_call x2, Pallas kernels, solve_call(): pl.pallas_call(kernel, out_shape=shapes[0] if single else shapes, in_spec...  28 us
    ppermute x11, waiting for transfers between devices, over_y(): return lax.ppermute(values, 'blk', SWAP_Y)  16.6 us
    ppermute x11, starting transfers between devices, over_y(): return lax.ppermute(values, 'blk', SWAP_Y)  16.1 us
    pallas_call x3, Pallas kernels, tile_call(): pl.pallas_call(functools.partial(tile_kernel, exponent_scale, len(halves)...  10.6 us
    ppermute x4, starting transfers between devices, panel(): outers[i] = lax.ppermute(panels[i], 'dp', TO_INNER)  9.87 us
    ppermute x4, waiting for transfers between devices, total(): givens[i] = lax.ppermute(totals[i], 'dp', TO_OUTER)  7.57 us
    dot_general x8, matrix products, part_of(): lax.dot_general(tile, centred, (((0,), (0,)), ((), ())), preferred_elemen...  6.18 us
    ppermute x4, starting transfers between devices, total(): givens[i] = lax.ppermute(totals[i], 'dp', TO_OUTER)  5.39 us
  transfers between devices with their start and end apart: 36, of which 18 were waited for; matrix products, arithmetic and copies ran while one was open for 14% of the time, Pallas kernels for 18%

profile of v3, /device:TPU:0, one launch (start us, length us, event | category | flops | bytes accessed | tf_op | source)
XLA Modules:
  0.0 144.7 jit_solution(11719548343147906938)
XLA Ops:
  1.6 2.7 %collective-permute-start.1 = (bf16[512,384]{1,0:T(8,128)(2,1)S(1)}, bf16[512,384]{1,0:T(8,128)(2,1)S(1)}, u32[]{:S(2)}, u32[]{:S(2)}) collective-permute-start(bf16[512,384]{1,0:T(8,128)(2,1)S(1)} %slice_select_fusion.1), channel_id=1, source_target_pairs={{0,8},{8,0},{4,12},{12,4},{1,9},{9,1},{5,13},{13,5},{2,10},{10,2},... | collective-permute-start | bytes 1179656 | tf_op jit(solution)/shard_map/ppermute | solution.py:325
  4.5 2.2 %collective-permute-start.2 = (bf16[512,384]{1,0:T(8,128)(2,1)S(1)}, bf16[512,384]{1,0:T(8,128)(2,1)S(1)}, u32[]{:S(2)}, u32[]{:S(2)}) collective-permute-start(bf16[512,384]{1,0:T(8,128)(2,1)S(1)} %slice_select_fusion), channel_id=1, source_target_pairs={{0,8},{8,0},{4,12},{12,4},{1,9},{9,1},{5,13},{13,5},{2,10},{10,2},... | collective-permute-start | bytes 1179656 | tf_op jit(solution)/shard_map/ppermute | solution.py:325
  6.7 2.0 %fusion = f32[1920]{0:T(1024)S(1)} fusion(bf16[960,768]{1,0:T(8,128)(2,1)} %collective-permute-done, bf16[960,768]{1,0:T(8,128)(2,1)S(1)} %copy-done.2), kind=kLoop, calls=%fused_computation.2 | loop fusion | flops 8845440 | bytes 2956800 | tf_op jit(solution)/shard_map/reduce_sum | solution.py:27
  8.7 2.5 %fusion.1.data_ref = bf16[1920,768]{1,0:T(8,128)(2,1)S(1)} fusion(f32[1920]{0:T(1024)S(1)} %add_rsqrt_fusion, bf16[960,768]{1,0:T(8,128)(2,1)} %collective-permute-done, bf16[960,768]{1,0:T(8,128)(2,1)S(1)} %copy-done.2), kind=kLoop, calls=%fused_computation.3 | loop fusion | flops 8847360 | bytes 5905920 | tf_op jit(solution)/shard_map/convert_element_type | solution.py:27
  11.3 5.0 %shard_map.37 = (bf16[1920,1024]{1,0:T(8,128)(2,1)S(1)}, f32[2,1024]{1,0:T(2,128)S(1)}) custom-call(bf16[1920,768]{1,0:T(8,128)(2,1)S(1)} %fusion.1.data_ref, s32[1]{0:T(128)} %bitcast.odd_ref, bf16[1024,768]{1,0:T(8,128)(2,1)S(1)} %copy-done.1), custom_call_target="tpu_custom_call" | custom-call | flops 3019898880 | bytes 6881280 | tf_op jit(solution)/shard_map/pallas_call | solution.py:302
  16.2 1.6 %collective-permute-start.3 = (bf16[512,384]{1,0:T(8,128)(2,1)S(1)}, bf16[512,384]{1,0:T(8,128)(2,1)S(1)}, u32[]{:S(2)}, u32[]{:S(2)}) collective-permute-start(bf16[512,384]{1,0:T(8,128)(2,1)S(1)} %collective-permute-done.1.refs_0_), channel_id=1, source_target_pairs={{0,1},{1,0},{2,3},{3,2},{4,5},{5,4},{6,7},{7,6},{8,9},{9,8},{10,11... | collective-permute-start | bytes 1179656 | tf_op jit(solution)/shard_map/ppermute | solution.py:422
  20.9 1.6 %collective-permute-start.4 = (bf16[1024,256]{1,0:T(8,128)(2,1)S(1)}, bf16[1024,256]{1,0:T(8,128)(2,1)S(1)}, u32[]{:S(2)}, u32[]{:S(2)}) collective-permute-start(bf16[1024,256]{1,0:T(8,128)(2,1)S(1)} %get-tuple-element.64), channel_id=1, source_target_pairs={{0,8},{8,0},{4,12},{12,4},{1,9},{9,1},{5,13},{13,5},{2,10},{10,2},... | collective-permute-start | bytes 1572872 | tf_op jit(solution)/shard_map/ppermute | solution.py:325
  22.7 2.0 %collective-permute-start.6 = (bf16[512,384]{1,0:T(8,128)(2,1)S(1)}, bf16[512,384]{1,0:T(8,128)(2,1)S(1)}, u32[]{:S(2)}, u32[]{:S(2)}) collective-permute-start(bf16[512,384]{1,0:T(8,128)(2,1)S(1)} %collective-permute-done.2.refs_0_), channel_id=1, source_target_pairs={{0,1},{1,0},{2,3},{3,2},{4,5},{5,4},{6,7},{7,6},{8,9},{9,8},{10,11... | collective-permute-start | bytes 1179656 | tf_op jit(solution)/shard_map/ppermute | solution.py:422
  24.7 3.6 %collective-permute-done.3.refs_1_ = bf16[512,384]{1,0:T(8,128)(2,1)S(1)} collective-permute-done((bf16[512,384]{1,0:T(8,128)(2,1)S(1)}, bf16[512,384]{1,0:T(8,128)(2,1)S(1)}, u32[]{:S(2)}, u32[]{:S(2)}) %collective-permute-start.3) | collective-permute-done | bytes 393248 | tf_op jit(solution)/shard_map/ppermute | solution.py:422
  28.3 2.8 %shard_map.38 = (bf16[1920,512]{1,0:T(8,128)(2,1)S(1)}, f32[2,512]{1,0:T(2,128)S(1)}) custom-call(bf16[1920,768]{1,0:T(8,128)(2,1)S(1)} %fusion.1.data_ref, s32[1]{0:T(128)} %bitcast.odd_ref, bf16[512,384]{1,0:T(8,128)(2,1)S(1)} %collective-permute-done.1.refs_0_, bf16[512,384]{1,0:T(8,128)(2,1)S(1)} %collective-permute-done.3.refs_1_), custom_call_target="tpu_custom_call" | custom-call | flops 1509949440 | bytes 4915200 | tf_op jit(solution)/shard_map/pallas_call | solution.py:302
  31.1 3.0 %collective-permute-done.5.first_ref = bf16[1024,256]{1,0:T(8,128)(2,1)S(1)} collective-permute-done((bf16[1024,256]{1,0:T(8,128)(2,1)S(1)}, bf16[1024,256]{1,0:T(8,128)(2,1)S(1)}, u32[]{:S(2)}, u32[]{:S(2)}) %collective-permute-start.5) | collective-permute-done | bytes 524320 | tf_op jit(solution)/shard_map/ppermute | solution.py:325
  35.6 2.9 %shard_map.39 = (bf16[1920,512]{1,0:T(8,128)(2,1)S(1)}, f32[2,512]{1,0:T(2,128)S(1)}) custom-call(bf16[1920,768]{1,0:T(8,128)(2,1)S(1)} %fusion.1.data_ref, s32[1]{0:T(128)} %bitcast.odd_ref, bf16[512,384]{1,0:T(8,128)(2,1)S(1)} %collective-permute-done.2.refs_0_, bf16[512,384]{1,0:T(8,128)(2,1)S(1)} %collective-permute-done.6.refs_1_), custom_call_target="tpu_custom_call" | custom-call | flops 1509949440 | bytes 4915200 | tf_op jit(solution)/shard_map/pallas_call | solution.py:302
  38.6 1.6 %collective-permute-start.7 = (f32[2,2048]{1,0:T(2,128)S(1)}, f32[2,2048]{1,0:T(2,128)S(1)}, u32[]{:S(2)}, u32[]{:S(2)}) collective-permute-start(f32[2,2048]{1,0:T(2,128)S(1)} %constant_dynamic-update-slice_fusion), channel_id=1, source_target_pairs={{0,1},{1,0},{2,3},{3,2},{4,5},{5,4},{6,7},{7,6},{8,9},{9,8},{10,11... | collective-permute-start | bytes 49160 | tf_op jit(solution)/shard_map/ppermute | solution.py:463
  40.2 2.6 %collective-permute-start.8 = (f32[2,2048]{1,0:T(2,128)S(1)}, f32[2,2048]{1,0:T(2,128)S(1)}, u32[]{:S(2)}, u32[]{:S(2)}) collective-permute-start(f32[2,2048]{1,0:T(2,128)S(1)} %constant_dynamic-update-slice_fusion), channel_id=1, source_target_pairs={{0,2},{2,0},{1,3},{3,1},{4,6},{6,4},{5,7},{7,5},{8,10},{10,8},{9,1... | collective-permute-start | bytes 49160 | tf_op jit(solution)/shard_map/ppermute | solution.py:463
  44.9 3.4 %collective-permute-done.9 = f32[2,2048]{1,0:T(2,128)S(1)} collective-permute-done((f32[2,2048]{1,0:T(2,128)S(1)}, f32[2,2048]{1,0:T(2,128)S(1)}, u32[]{:S(2)}, u32[]{:S(2)}) %collective-permute-start.9) | collective-permute-done | bytes 16416 | tf_op jit(solution)/shard_map/ppermute | solution.py:463
  50.1 2.1 %collective-permute-done.10 = f32[2,2048]{1,0:T(2,128)S(1)} collective-permute-done((f32[2,2048]{1,0:T(2,128)S(1)}, f32[2,2048]{1,0:T(2,128)S(1)}, u32[]{:S(2)}, u32[]{:S(2)}) %collective-permute-start.10) | collective-permute-done | bytes 16416 | tf_op jit(solution)/shard_map/ppermute | solution.py:325
  59.2 5.8 %collective-permute-done.14 = f16[512,256]{1,0:T(8,128)(2,1)S(1)} collective-permute-done((f16[512,256]{1,0:T(8,128)(2,1)S(1)}, f16[512,256]{1,0:T(8,128)(2,1)S(1)}, u32[]{:S(2)}, u32[]{:S(2)}) %collective-permute-start.14) | collective-permute-done | bytes 262176 | tf_op jit(solution)/shard_map/ppermute | solution.py:325
  68.9 1.6 %collective-permute-done.17 = f16[512,256]{1,0:T(8,128)(2,1)S(1)} collective-permute-done((f16[512,256]{1,0:T(8,128)(2,1)S(1)}, f16[512,256]{1,0:T(8,128)(2,1)S(1)}, u32[]{:S(2)}, u32[]{:S(2)}) %collective-permute-start.17) | collective-permute-done | bytes 262176 | tf_op jit(solution)/shard_map/ppermute | solution.py:325
  71.3 1.3 collective-permute-start.21
  76.9 2.7 %collective-permute-start.18 = (f16[512,256]{1,0:T(8,128)(2,1)S(1)}, f16[512,256]{1,0:T(8,128)(2,1)S(1)}, u32[]{:S(2)}, u32[]{:S(2)}) collective-permute-start(f16[512,256]{1,0:T(8,128)(2,1)S(1)} %fusion.55), channel_id=1, source_target_pairs={{0,1},{3,2},{4,5},{7,6},{8,9},{11,10},{12,13},{15,14},{16,17},{19,... | collective-permute-start | bytes 786440 | tf_op jit(solution)/shard_map/ppermute | solution.py:535
  82.6 4.6 %collective-permute-start.23 = (f16[512,256]{1,0:T(8,128)(2,1)S(1)}, f16[512,256]{1,0:T(8,128)(2,1)S(1)}, u32[]{:S(2)}, u32[]{:S(2)}) collective-permute-start(f16[512,256]{1,0:T(8,128)(2,1)S(1)} %fusion.46), channel_id=1, source_target_pairs={{0,1},{3,2},{4,5},{7,6},{8,9},{11,10},{12,13},{15,14},{16,17},{19,... | collective-permute-start | bytes 786440 | tf_op jit(solution)/shard_map/ppermute | solution.py:535
  89.4 1.7 %collective-permute-done.23 = f16[512,256]{1,0:T(8,128)(2,1)S(1)} collective-permute-done((f16[512,256]{1,0:T(8,128)(2,1)S(1)}, f16[512,256]{1,0:T(8,128)(2,1)S(1)}, u32[]{:S(2)}, u32[]{:S(2)}) %collective-permute-start.23) | collective-permute-done | bytes 262176 | tf_op jit(solution)/shard_map/ppermute | solution.py:535
  93.4 3.7 %collective-permute-done.27 = f16[512,256]{1,0:T(8,128)(2,1)S(1)} collective-permute-done((f16[512,256]{1,0:T(8,128)(2,1)S(1)}, f16[512,256]{1,0:T(8,128)(2,1)S(1)}, u32[]{:S(2)}, u32[]{:S(2)}) %collective-permute-start.27) | collective-permute-done | bytes 262176 | tf_op jit(solution)/shard_map/ppermute | solution.py:543
  98.6 1.5 %collective-permute-start.30 = (f16[512,256]{1,0:T(8,128)(2,1)S(1)}, f16[512,256]{1,0:T(8,128)(2,1)S(1)}, u32[]{:S(2)}, u32[]{:S(2)}) collective-permute-start(f16[512,256]{1,0:T(8,128)(2,1)S(1)} %add_convert_fusion), channel_id=1, source_target_pairs={{1,0},{2,3},{5,4},{6,7},{9,8},{10,11},{13,12},{14,15},{17,16},{18,... | collective-permute-start | bytes 786440 | tf_op jit(solution)/shard_map/ppermute | solution.py:543
  100.2 1.9 %collective-permute-start.31 = (f32[128,256]{1,0:T(8,128)S(1)}, f32[128,256]{1,0:T(8,128)S(1)}, u32[]{:S(2)}, u32[]{:S(2)}) collective-permute-start(f32[128,256]{1,0:T(8,128)S(1)} %select_add_fusion.1), channel_id=1, source_target_pairs={{0,8},{8,0},{4,12},{12,4},{1,9},{9,1},{5,13},{13,5},{2,10},{10,2},... | collective-permute-start | bytes 393224 | tf_op jit(solution)/shard_map/ppermute | solution.py:325
  103.1 3.1 %collective-permute-done.31 = f32[128,256]{1,0:T(8,128)S(1)} collective-permute-done((f32[128,256]{1,0:T(8,128)S(1)}, f32[128,256]{1,0:T(8,128)S(1)}, u32[]{:S(2)}, u32[]{:S(2)}) %collective-permute-start.31) | collective-permute-done | bytes 131104 | tf_op jit(solution)/shard_map/ppermute | solution.py:325
  106.2 3.0 %collective-permute-done.30 = f16[512,256]{1,0:T(8,128)(2,1)S(1)} collective-permute-done((f16[512,256]{1,0:T(8,128)(2,1)S(1)}, f16[512,256]{1,0:T(8,128)(2,1)S(1)}, u32[]{:S(2)}, u32[]{:S(2)}) %collective-permute-start.30) | collective-permute-done | bytes 262176 | tf_op jit(solution)/shard_map/ppermute | solution.py:543
  109.3 2.0 %fusion.2 = f32[256,512]{1,0:T(8,128)S(1)} fusion(f32[512,256]{1,0:T(8,128)S(1)} %convert_multiply_fusion.2, f32[512,256]{1,0:T(8,128)S(1)} %convert_multiply_fusion.3, f32[512,256]{1,0:T(8,128)S(1)} %convert_multiply_fusion.4.lower_ref, f32[512,256]{1,0:T(8,128)S(1)} %convert_multiply_fusion.5.upper_ref), kind=kOutput, calls=%fused_computation.9 | convolution fusion | flops 1612447744 | bytes 2621440 | tf_op jit(solution)/shard_map/dot_general | solution.py:333
  113.0 1.9 %collective-permute-start.33 = (f32[128,512]{1,0:T(8,128)S(1)}, f32[128,512]{1,0:T(8,128)S(1)}, u32[]{:S(2)}, u32[]{:S(2)}) collective-permute-start(f32[128,512]{1,0:T(8,128)S(1)} %select_add_fusion), channel_id=1, source_target_pairs={{0,8},{8,0},{4,12},{12,4},{1,9},{9,1},{5,13},{13,5},{2,10},{10,2},... | collective-permute-start | bytes 786440 | tf_op jit(solution)/shard_map/ppermute | solution.py:325
  114.9 12.8 %shard_map.42 = (f32[1024,256]{1,0:T(8,128)S(1)}, f32[256,256]{1,0:T(8,128)S(1)}) custom-call(f32[256,256]{1,0:T(8,128)S(1)} %pad_maximum_fusion.5.gram_ref, f32[1024,256]{1,0:T(8,128)S(1)} %pad_maximum_fusion.2.rows_ref), custom_call_target="tpu_custom_call" | custom-call | flops 13421772800 | bytes 1310720 | tf_op jit(solution)/shard_map/pallas_call | solution.py:184
  128.0 1.4 collective-permute-done.35
  129.5 15.2 %shard_map.43 = f32[1024,512]{1,0:T(8,128)} custom-call(f32[256,512]{1,0:T(8,128)S(1)} %pad_maximum_fusion.3.gram_ref, f32[1024,256]{1,0:T(8,128)S(1)} %pad_maximum_fusion.1.rows_ref, f32[1024,256]{1,0:T(8,128)S(1)} %get-tuple-element.102.done_ref, f32[256,256]{1,0:T(8,128)S(1)} %get-tuple-element.104.solve_ref), custom_call_target="tpu_custom_call" | custom-call | flops 10737418240 | bytes 1048576 | tf_op jit(solution)/shard_map/pallas_call | solution.py:184
  (116 shorter events, 38.4 us)
Async XLA Ops:
  0.0 4.4 %collective-permute-start = (bf16[960,768]{1,0:T(8,128)(2,1)}, bf16[960,768]{1,0:T(8,128)(2,1)}, u32[]{:S(2)}, u32[]{:S(2)}) collective-permute-start(bf16[960,768]{1,0:T(8,128)(2,1)} %param.3), channel_id=1, source_target_pairs={{0,4},{4,0},{8,12},{12,8},{1,5},{5,1},{9,13},{13,9},{2,6},{6,2},{1... | collective-permute-start | bytes 4423688 | tf_op jit(solution)/shard_map/ppermute | solution.py:321
  1.6 14.6 %collective-permute-start.1 = (bf16[512,384]{1,0:T(8,128)(2,1)S(1)}, bf16[512,384]{1,0:T(8,128)(2,1)S(1)}, u32[]{:S(2)}, u32[]{:S(2)}) collective-permute-start(bf16[512,384]{1,0:T(8,128)(2,1)S(1)} %slice_select_fusion.1), channel_id=1, source_target_pairs={{0,8},{8,0},{4,12},{12,4},{1,9},{9,1},{5,13},{13,5},{2,10},{10,2},... | collective-permute-start | bytes 1179656 | tf_op jit(solution)/shard_map/ppermute | solution.py:325
  4.5 18.2 %collective-permute-start.2 = (bf16[512,384]{1,0:T(8,128)(2,1)S(1)}, bf16[512,384]{1,0:T(8,128)(2,1)S(1)}, u32[]{:S(2)}, u32[]{:S(2)}) collective-permute-start(bf16[512,384]{1,0:T(8,128)(2,1)S(1)} %slice_select_fusion), channel_id=1, source_target_pairs={{0,8},{8,0},{4,12},{12,4},{1,9},{9,1},{5,13},{13,5},{2,10},{10,2},... | collective-permute-start | bytes 1179656 | tf_op jit(solution)/shard_map/ppermute | solution.py:325
  16.2 12.1 %collective-permute-start.3 = (bf16[512,384]{1,0:T(8,128)(2,1)S(1)}, bf16[512,384]{1,0:T(8,128)(2,1)S(1)}, u32[]{:S(2)}, u32[]{:S(2)}) collective-permute-start(bf16[512,384]{1,0:T(8,128)(2,1)S(1)} %collective-permute-done.1.refs_0_), channel_id=1, source_target_pairs={{0,1},{1,0},{2,3},{3,2},{4,5},{5,4},{6,7},{7,6},{8,9},{9,8},{10,11... | collective-permute-start | bytes 1179656 | tf_op jit(solution)/shard_map/ppermute | solution.py:422
  19.1 14.9 %collective-permute-start.5 = (bf16[1024,256]{1,0:T(8,128)(2,1)S(1)}, bf16[1024,256]{1,0:T(8,128)(2,1)S(1)}, u32[]{:S(2)}, u32[]{:S(2)}) collective-permute-start(bf16[1024,256]{1,0:T(8,128)(2,1)S(1)} %get-tuple-element.67), channel_id=1, source_target_pairs={{0,8},{8,0},{4,12},{12,4},{1,9},{9,1},{5,13},{13,5},{2,10},{10,2},... | collective-permute-start | bytes 1572872 | tf_op jit(solution)/shard_map/ppermute | solution.py:325
  20.9 27.4 %collective-permute-start.4 = (bf16[1024,256]{1,0:T(8,128)(2,1)S(1)}, bf16[1024,256]{1,0:T(8,128)(2,1)S(1)}, u32[]{:S(2)}, u32[]{:S(2)}) collective-permute-start(bf16[1024,256]{1,0:T(8,128)(2,1)S(1)} %get-tuple-element.64), channel_id=1, source_target_pairs={{0,8},{8,0},{4,12},{12,4},{1,9},{9,1},{5,13},{13,5},{2,10},{10,2},... | collective-permute-start | bytes 1572872 | tf_op jit(solution)/shard_map/ppermute | solution.py:325
  22.7 12.9 %collective-permute-start.6 = (bf16[512,384]{1,0:T(8,128)(2,1)S(1)}, bf16[512,384]{1,0:T(8,128)(2,1)S(1)}, u32[]{:S(2)}, u32[]{:S(2)}) collective-permute-start(bf16[512,384]{1,0:T(8,128)(2,1)S(1)} %collective-permute-done.2.refs_0_), channel_id=1, source_target_pairs={{0,1},{1,0},{2,3},{3,2},{4,5},{5,4},{6,7},{7,6},{8,9},{9,8},{10,11... | collective-permute-start | bytes 1179656 | tf_op jit(solution)/shard_map/ppermute | solution.py:422
  38.6 5.2 %collective-permute-start.7 = (f32[2,2048]{1,0:T(2,128)S(1)}, f32[2,2048]{1,0:T(2,128)S(1)}, u32[]{:S(2)}, u32[]{:S(2)}) collective-permute-start(f32[2,2048]{1,0:T(2,128)S(1)} %constant_dynamic-update-slice_fusion), channel_id=1, source_target_pairs={{0,1},{1,0},{2,3},{3,2},{4,5},{5,4},{6,7},{7,6},{8,9},{9,8},{10,11... | collective-permute-start | bytes 49160 | tf_op jit(solution)/shard_map/ppermute | solution.py:463
  40.2 4.7 %collective-permute-start.8 = (f32[2,2048]{1,0:T(2,128)S(1)}, f32[2,2048]{1,0:T(2,128)S(1)}, u32[]{:S(2)}, u32[]{:S(2)}) collective-permute-start(f32[2,2048]{1,0:T(2,128)S(1)} %constant_dynamic-update-slice_fusion), channel_id=1, source_target_pairs={{0,2},{2,0},{1,3},{3,1},{4,6},{6,4},{5,7},{7,5},{8,10},{10,8},{9,1... | collective-permute-start | bytes 49160 | tf_op jit(solution)/shard_map/ppermute | solution.py:463
  42.8 5.5 %collective-permute-start.9 = (f32[2,2048]{1,0:T(2,128)S(1)}, f32[2,2048]{1,0:T(2,128)S(1)}, u32[]{:S(2)}, u32[]{:S(2)}) collective-permute-start(f32[2,2048]{1,0:T(2,128)S(1)} %constant_dynamic-update-slice_fusion), channel_id=1, source_target_pairs={{0,3},{3,0},{1,2},{2,1},{4,7},{7,4},{5,6},{6,5},{8,11},{11,8},{9,1... | collective-permute-start | bytes 49160 | tf_op jit(solution)/shard_map/ppermute | solution.py:463
  43.7 10.8 %collective-permute-start.13 = (f32[1920,256]{1,0:T(8,128)S(1)}, f32[1920,256]{1,0:T(8,128)S(1)}, u32[]{:S(2)}, u32[]{:S(2)}) collective-permute-start(f32[1920,256]{1,0:T(8,128)S(1)} %convolution_add_fusion), channel_id=1, source_target_pairs={{0,4},{4,0},{8,12},{12,8},{1,5},{5,1},{9,13},{13,9},{2,6},{6,2},{1... | collective-permute-start | bytes 5898248 | tf_op jit(solution)/shard_map/ppermute | solution.py:321
  48.4 3.8 %collective-permute-start.10 = (f32[2,2048]{1,0:T(2,128)S(1)}, f32[2,2048]{1,0:T(2,128)S(1)}, u32[]{:S(2)}, u32[]{:S(2)}) collective-permute-start(f32[2,2048]{1,0:T(2,128)S(1)} %pad_maximum_fusion.6), channel_id=1, source_target_pairs={{0,8},{8,0},{4,12},{12,4},{1,9},{9,1},{5,13},{13,5},{2,10},{10,2},... | collective-permute-start | bytes 49160 | tf_op jit(solution)/shard_map/ppermute | solution.py:325
  54.2 4.6 %collective-permute-start.12 = (f32[1920,256]{1,0:T(8,128)S(1)}, f32[1920,256]{1,0:T(8,128)S(1)}, u32[]{:S(2)}, u32[]{:S(2)}) collective-permute-start(f32[1920,256]{1,0:T(8,128)S(1)} %convolution_add_fusion.2), channel_id=1, source_target_pairs={{0,4},{4,0},{8,12},{12,8},{1,5},{5,1},{9,13},{13,9},{2,6},{6,2},{1... | collective-permute-start | bytes 5898248 | tf_op jit(solution)/shard_map/ppermute | solution.py:321
  55.8 9.2 %collective-permute-start.14 = (f16[512,256]{1,0:T(8,128)(2,1)S(1)}, f16[512,256]{1,0:T(8,128)(2,1)S(1)}, u32[]{:S(2)}, u32[]{:S(2)}) collective-permute-start(f16[512,256]{1,0:T(8,128)(2,1)S(1)} %fusion.58), channel_id=1, source_target_pairs={{0,8},{8,0},{4,12},{12,4},{1,9},{9,1},{5,13},{13,5},{2,10},{10,2},... | collective-permute-start | bytes 786440 | tf_op jit(solution)/shard_map/ppermute | solution.py:325
  57.6 12.9 %collective-permute-start.17 = (f16[512,256]{1,0:T(8,128)(2,1)S(1)}, f16[512,256]{1,0:T(8,128)(2,1)S(1)}, u32[]{:S(2)}, u32[]{:S(2)}) collective-permute-start(f16[512,256]{1,0:T(8,128)(2,1)S(1)} %fusion.59), channel_id=1, source_target_pairs={{0,8},{8,0},{4,12},{12,4},{1,9},{9,1},{5,13},{13,5},{2,10},{10,2},... | collective-permute-start | bytes 786440 | tf_op jit(solution)/shard_map/ppermute | solution.py:325
  65.8 8.7 %collective-permute-start.16 = (f16[512,256]{1,0:T(8,128)(2,1)S(1)}, f16[512,256]{1,0:T(8,128)(2,1)S(1)}, u32[]{:S(2)}, u32[]{:S(2)}) collective-permute-start(f16[512,256]{1,0:T(8,128)(2,1)S(1)} %fusion.52), channel_id=1, source_target_pairs={{0,1},{3,2},{4,5},{7,6},{8,9},{11,10},{12,13},{15,14},{16,17},{19,... | collective-permute-start | bytes 786440 | tf_op jit(solution)/shard_map/ppermute | solution.py:535
  67.8 8.3 %collective-permute-start.15 = (f16[512,256]{1,0:T(8,128)(2,1)S(1)}, f16[512,256]{1,0:T(8,128)(2,1)S(1)}, u32[]{:S(2)}, u32[]{:S(2)}) collective-permute-start(f16[512,256]{1,0:T(8,128)(2,1)S(1)} %fusion.60), channel_id=1, source_target_pairs={{0,8},{8,0},{4,12},{12,4},{1,9},{9,1},{5,13},{13,5},{2,10},{10,2},... | collective-permute-start | bytes 786440 | tf_op jit(solution)/shard_map/ppermute | solution.py:325
  71.3 8.3 %collective-permute-start.21 = (f16[512,256]{1,0:T(8,128)(2,1)S(1)}, f16[512,256]{1,0:T(8,128)(2,1)S(1)}, u32[]{:S(2)}, u32[]{:S(2)}) collective-permute-start(f16[512,256]{1,0:T(8,128)(2,1)S(1)} %fusion.49), channel_id=1, source_target_pairs={{0,1},{3,2},{4,5},{7,6},{8,9},{11,10},{12,13},{15,14},{16,17},{19,... | collective-permute-start | bytes 786440 | tf_op jit(solution)/shard_map/ppermute | solution.py:535
  73.4 8.4 %collective-permute-start.19 = (f16[512,256]{1,0:T(8,128)(2,1)S(1)}, f16[512,256]{1,0:T(8,128)(2,1)S(1)}, u32[]{:S(2)}, u32[]{:S(2)}) collective-permute-start(f16[512,256]{1,0:T(8,128)(2,1)S(1)} %fusion.61), channel_id=1, source_target_pairs={{0,8},{8,0},{4,12},{12,4},{1,9},{9,1},{5,13},{13,5},{2,10},{10,2},... | collective-permute-start | bytes 786440 | tf_op jit(solution)/shard_map/ppermute | solution.py:325
  74.5 5.9 %collective-permute-start.20 = (f16[512,256]{1,0:T(8,128)(2,1)S(1)}, f16[512,256]{1,0:T(8,128)(2,1)S(1)}, u32[]{:S(2)}, u32[]{:S(2)}) collective-permute-start(f16[512,256]{1,0:T(8,128)(2,1)S(1)} %add_convert_fusion.7), channel_id=1, source_target_pairs={{1,2},{2,1},{5,6},{6,5},{9,10},{10,9},{13,14},{14,13},{17,18},{18,... | collective-permute-start | bytes 786440 | tf_op jit(solution)/shard_map/ppermute | solution.py:539
  76.9 10.3 %collective-permute-start.18 = (f16[512,256]{1,0:T(8,128)(2,1)S(1)}, f16[512,256]{1,0:T(8,128)(2,1)S(1)}, u32[]{:S(2)}, u32[]{:S(2)}) collective-permute-start(f16[512,256]{1,0:T(8,128)(2,1)S(1)} %fusion.55), channel_id=1, source_target_pairs={{0,1},{3,2},{4,5},{7,6},{8,9},{11,10},{12,13},{15,14},{16,17},{19,... | collective-permute-start | bytes 786440 | tf_op jit(solution)/shard_map/ppermute | solution.py:535
  79.7 8.3 %collective-permute-start.24 = (f16[512,256]{1,0:T(8,128)(2,1)S(1)}, f16[512,256]{1,0:T(8,128)(2,1)S(1)}, u32[]{:S(2)}, u32[]{:S(2)}) collective-permute-start(f16[512,256]{1,0:T(8,128)(2,1)S(1)} %add_convert_fusion.6), channel_id=1, source_target_pairs={{1,2},{2,1},{5,6},{6,5},{9,10},{10,9},{13,14},{14,13},{17,18},{18,... | collective-permute-start | bytes 786440 | tf_op jit(solution)/shard_map/ppermute | solution.py:539
  80.5 12.7 %collective-permute-start.26 = (f16[512,256]{1,0:T(8,128)(2,1)S(1)}, f16[512,256]{1,0:T(8,128)(2,1)S(1)}, u32[]{:S(2)}, u32[]{:S(2)}) collective-permute-start(f16[512,256]{1,0:T(8,128)(2,1)S(1)} %add_convert_fusion.5), channel_id=1, source_target_pairs={{1,0},{2,3},{5,4},{6,7},{9,8},{10,11},{13,12},{14,15},{17,16},{18,... | collective-permute-start | bytes 786440 | tf_op jit(solution)/shard_map/ppermute | solution.py:543
  82.6 8.4 %collective-permute-start.23 = (f16[512,256]{1,0:T(8,128)(2,1)S(1)}, f16[512,256]{1,0:T(8,128)(2,1)S(1)}, u32[]{:S(2)}, u32[]{:S(2)}) collective-permute-start(f16[512,256]{1,0:T(8,128)(2,1)S(1)} %fusion.46), channel_id=1, source_target_pairs={{0,1},{3,2},{4,5},{7,6},{8,9},{11,10},{12,13},{15,14},{16,17},{19,... | collective-permute-start | bytes 786440 | tf_op jit(solution)/shard_map/ppermute | solution.py:535
  87.3 4.5 %collective-permute-start.22 = (f16[512,256]{1,0:T(8,128)(2,1)S(1)}, f16[512,256]{1,0:T(8,128)(2,1)S(1)}, u32[]{:S(2)}, u32[]{:S(2)}) collective-permute-start(f16[512,256]{1,0:T(8,128)(2,1)S(1)} %add_convert_fusion.4), channel_id=1, source_target_pairs={{1,2},{2,1},{5,6},{6,5},{9,10},{10,9},{13,14},{14,13},{17,18},{18,... | collective-permute-start | bytes 786440 | tf_op jit(solution)/shard_map/ppermute | solution.py:539
  88.1 9.0 %collective-permute-start.27 = (f16[512,256]{1,0:T(8,128)(2,1)S(1)}, f16[512,256]{1,0:T(8,128)(2,1)S(1)}, u32[]{:S(2)}, u32[]{:S(2)}) collective-permute-start(f16[512,256]{1,0:T(8,128)(2,1)S(1)} %add_convert_fusion.3), channel_id=1, source_target_pairs={{1,0},{2,3},{5,4},{6,7},{9,8},{10,11},{13,12},{14,15},{17,16},{18,... | collective-permute-start | bytes 786440 | tf_op jit(solution)/shard_map/ppermute | solution.py:543
  91.1 7.4 %collective-permute-start.29 = (f16[512,256]{1,0:T(8,128)(2,1)S(1)}, f16[512,256]{1,0:T(8,128)(2,1)S(1)}, u32[]{:S(2)}, u32[]{:S(2)}) collective-permute-start(f16[512,256]{1,0:T(8,128)(2,1)S(1)} %add_convert_fusion.2), channel_id=1, source_target_pairs={{1,2},{2,1},{5,6},{6,5},{9,10},{10,9},{13,14},{14,13},{17,18},{18,... | collective-permute-start | bytes 786440 | tf_op jit(solution)/shard_map/ppermute | solution.py:539
  91.9 11.0 %collective-permute-start.25 = (f16[512,256]{1,0:T(8,128)(2,1)S(1)}, f16[512,256]{1,0:T(8,128)(2,1)S(1)}, u32[]{:S(2)}, u32[]{:S(2)}) collective-permute-start(f16[512,256]{1,0:T(8,128)(2,1)S(1)} %add_convert_fusion.1), channel_id=1, source_target_pairs={{1,0},{2,3},{5,4},{6,7},{9,8},{10,11},{13,12},{14,15},{17,16},{18,... | collective-permute-start | bytes 786440 | tf_op jit(solution)/shard_map/ppermute | solution.py:543
  98.6 10.6 %collective-permute-start.30 = (f16[512,256]{1,0:T(8,128)(2,1)S(1)}, f16[512,256]{1,0:T(8,128)(2,1)S(1)}, u32[]{:S(2)}, u32[]{:S(2)}) collective-permute-start(f16[512,256]{1,0:T(8,128)(2,1)S(1)} %add_convert_fusion), channel_id=1, source_target_pairs={{1,0},{2,3},{5,4},{6,7},{9,8},{10,11},{13,12},{14,15},{17,16},{18,... | collective-permute-start | bytes 786440 | tf_op jit(solution)/shard_map/ppermute | solution.py:543
  100.2 6.0 %collective-permute-start.31 = (f32[128,256]{1,0:T(8,128)S(1)}, f32[128,256]{1,0:T(8,128)S(1)}, u32[]{:S(2)}, u32[]{:S(2)}) collective-permute-start(f32[128,256]{1,0:T(8,128)S(1)} %select_add_fusion.1), channel_id=1, source_target_pairs={{0,8},{8,0},{4,12},{12,4},{1,9},{9,1},{5,13},{13,5},{2,10},{10,2},... | collective-permute-start | bytes 393224 | tf_op jit(solution)/shard_map/ppermute | solution.py:325
  111.5 3.4 %collective-permute-start.34 = (f32[128,256]{1,0:T(8,128)S(1)}, f32[128,256]{1,0:T(8,128)S(1)}, u32[]{:S(2)}, u32[]{:S(2)}) collective-permute-start(f32[128,256]{1,0:T(8,128)S(1)} %add.128), channel_id=1, source_target_pairs={{0,4},{4,0},{8,12},{12,8},{1,5},{5,1},{9,13},{13,9},{2,6},{6,2},{1... | collective-permute-start | bytes 393224 | tf_op jit(solution)/shard_map/ppermute | solution.py:321
  113.0 14.8 %collective-permute-start.33 = (f32[128,512]{1,0:T(8,128)S(1)}, f32[128,512]{1,0:T(8,128)S(1)}, u32[]{:S(2)}, u32[]{:S(2)}) collective-permute-start(f32[128,512]{1,0:T(8,128)S(1)} %select_add_fusion), channel_id=1, source_target_pairs={{0,8},{8,0},{4,12},{12,4},{1,9},{9,1},{5,13},{13,5},{2,10},{10,2},... | collective-permute-start | bytes 786440 | tf_op jit(solution)/shard_map/ppermute | solution.py:325
  (8 other events, 18.1 us)
